TPU v7x, 256 devices: a whole 4x4x8 slice. The times are simulated.
256 devices in a mesh: req: 64 (over y_hi, z, x), blk: 4 (over y_lo, core).
Axes of the slice: x: 4, y: 4 (y_hi: 2, y_lo: 2; y = y_hi * 2 + y_lo), z: 8, core: 2. Of those that a mesh axis runs over, the one named last changes fastest.
Arguments:
- queries: bfloat16 [2, 128, 8192], P(None, 'req'), may hold values from -96 to 96
- new_keys: bfloat16 [2, 128, 1024], P(None, 'req'), may hold values from -4.6 to 4.6
- new_values: bfloat16 [2, 128, 1024], P(None, 'req'), may hold values from -5 to 5
- cache: bfloat16 [128, 64, 16, 2048], P('req', 'blk'), may hold values from -5 to 5
- page_table: int32 [128, 64], P('req'), may hold values from 0 to 63, as said below
- kept: int32 [2, 128, 8, 16], P(None, 'req'), may hold values from 0 to 63, as said below
- moves: int32 [64], replicated, may hold values from 0 to 63, as said below
Outputs:
- first_out: bfloat16 [128, 8192], P('req', 'blk')
- second_out: bfloat16 [128, 8192], P('req', 'blk')
- cache_after: bfloat16 [128, 64, 16, 2048], P('req', 'blk')
Inputs may be any that keep to these rules, and one draw needn't show every extreme that they name: `page_table`: each row is a permutation of the 64 storage positions. `kept`: each list of 16 ids is distinct; through page_table at most 8 of them lie in one index of blk's storage block of 16 positions, and exactly 8 in some block. moves[moves[g]] = g; every g with moves[g] != g has moves[g] = g XOR a distance common to all such g; moves[0] != 0.
All inputs are finite; a program needn't handle non-finite values.
Results may differ from a plain program's by a relative error of at most 0.013.
Values may be sent and summed in bfloat16 or wider, within the bound.
A program may use at most 64 MiB of HBM per device.

v0:
```python
import jax
import jax.numpy as jnp
from jax import lax
from jax.sharding import PartitionSpec as P

neg_large = -1e30


def joined(array, axis, combine):
    everything = jax.tree.map(
        lambda part, kind: lax.all_gather(part.astype(kind), axis),
        array,
        (jnp.bfloat16, jnp.bfloat16, jnp.bfloat16),
    )

    def take(k):
        return jax.tree.map(lambda part, own: part[k].astype(own.dtype), everything, array)

    return lax.fori_loop(
        1, lax.axis_size(axis), lambda k, so_far: combine(so_far, take(k)), take(0)
    )


def swapped(array, axis, distance):
    return lax.ppermute(array, axis, [(i, i ^ 1 << distance) for i in range(lax.axis_size(axis))])


def combine(first, second):
    top_first, total_first, weighted_first = first
    top_second, total_second, weighted_second = second
    top_score = jnp.maximum(top_first, top_second)
    factor_first = jnp.exp(top_first - top_score)
    factor_second = jnp.exp(top_second - top_score)
    total = total_first * factor_first + total_second * factor_second
    weighted = weighted_first * factor_first[..., None] + weighted_second * factor_second[..., None]
    return (top_score, total, weighted)


def local_partials(
    query_rows, kept_rows, table, cache_rows, blk_index, capacity, kv_heads, head_size
):
    score_scale = head_size ** (-0.5)
    row_count = cache_rows.shape[0]
    block_pages = cache_rows.shape[1]
    page_size = cache_rows.shape[2]
    page_locs = jax.vmap(lambda row_table, row_kept: row_table[row_kept])(table, kept_rows)
    stored_here = page_locs // block_pages == blk_index
    slot_ids = page_locs % block_pages
    local_rank = jnp.cumsum(stored_here.astype(jnp.int32), axis=-1) - 1
    select = (
        local_rank[:, :, None, :] == jnp.arange(capacity, dtype=jnp.int32)[None, None, :, None]
    ) & stored_here[:, :, None, :]
    slot_pick = jnp.sum(jnp.where(select, slot_ids[:, :, None, :], 0), axis=-1)
    usable = jnp.any(select, axis=-1)
    paged_view = cache_rows.reshape(row_count, block_pages, page_size, 2, kv_heads, head_size)
    request_ids = jnp.arange(row_count, dtype=jnp.int32)[:, None, None]
    head_ids = jnp.arange(kv_heads, dtype=jnp.int32)[None, :, None]
    fetched = paged_view[request_ids, slot_pick, :, :, head_ids, :]
    cached_keys = fetched[:, :, :, :, 0, :].reshape(
        row_count, kv_heads, capacity * page_size, head_size
    )
    cached_values = fetched[:, :, :, :, 1, :].reshape(
        row_count, kv_heads, capacity * page_size, head_size
    )
    query_heads = query_rows.reshape(row_count, kv_heads, -1, head_size)
    scores = (
        jnp.einsum("rjgd,rjtd->rjgt", query_heads, cached_keys, preferred_element_type=jnp.float32)
        * score_scale
    )
    token_mask = jnp.repeat(usable, page_size, axis=-1)[:, :, None, :]
    scores = jnp.where(token_mask, scores, neg_large)
    top_score = jnp.max(scores, axis=-1)
    weights = jnp.where(token_mask, jnp.exp(scores - top_score[..., None]), 0.0)
    total = jnp.sum(weights, axis=-1)
    weighted = jnp.einsum(
        "rjgt,rjtd->rjgd",
        weights.astype(jnp.bfloat16),
        cached_values,
        preferred_element_type=jnp.float32,
    )
    return (top_score, total, weighted)


def finish_heads(
    top_score, total, weighted, query_own, fresh_keys, fresh_values, own_heads, head_size
):
    score_scale = head_size ** (-0.5)
    row_count = query_own.shape[0]
    steps_used = fresh_keys.shape[0]
    query_heads = query_own.reshape(row_count, own_heads, -1, head_size)
    key_heads = fresh_keys.reshape(steps_used, row_count, own_heads, head_size)
    value_heads = fresh_values.reshape(steps_used, row_count, own_heads, head_size)
    fresh_scores = (
        jnp.einsum("rjgd,nrjd->rjgn", query_heads, key_heads, preferred_element_type=jnp.float32)
        * score_scale
    )
    new_top = jnp.maximum(top_score, jnp.max(fresh_scores, axis=-1))
    factor = jnp.exp(top_score - new_top)
    fresh_weights = jnp.exp(fresh_scores - new_top[..., None])
    new_total = total * factor + jnp.sum(fresh_weights, axis=-1)
    mixed = weighted * factor[..., None]
    mixed = mixed + jnp.einsum(
        "rjgn,nrjd->rjgd",
        fresh_weights.astype(jnp.bfloat16),
        value_heads,
        preferred_element_type=jnp.float32,
    )
    return (mixed / new_total[..., None]).astype(jnp.bfloat16).reshape(row_count, -1)


def on_device(queries, new_keys, new_values, cache, page_table, kept, moves):
    blk_index = lax.axis_index("blk")
    blk_count = lax.axis_size("blk")
    req_index = lax.axis_index("req")
    req_count = lax.axis_size("req")
    kv_heads = kept.shape[2]
    own_heads = kv_heads // blk_count
    head_size = cache.shape[3] // (2 * kv_heads)
    query_width = own_heads * (queries.shape[2] // kv_heads)
    capacity = cache.shape[1] // 2

    def reduce_partials(partials):
        merged = joined((partials[0], partials[1], partials[2]), "blk", combine)
        return tuple(
            (
                lax.dynamic_slice_in_dim(piece, blk_index * own_heads, own_heads, 1)
                for piece in merged
            )
        )

    def attend(query_rows, key_rows, value_rows, table, kept_rows, cache_rows):
        partials = local_partials(
            query_rows, kept_rows, table, cache_rows, blk_index, capacity, kv_heads, head_size
        )
        top_score, total, weighted = reduce_partials(partials)
        query_own = lax.dynamic_slice_in_dim(query_rows, blk_index * query_width, query_width, 1)
        key_own = lax.dynamic_slice_in_dim(
            key_rows, blk_index * own_heads * head_size, own_heads * head_size, 2
        )
        value_own = lax.dynamic_slice_in_dim(
            value_rows, blk_index * own_heads * head_size, own_heads * head_size, 2
        )
        return finish_heads(
            top_score, total, weighted, query_own, key_own, value_own, own_heads, head_size
        )

    def hop_slot(payload, bit_number, taking):
        arrived = swapped((payload[0], payload[1], payload[2], payload[3]), "req", bit_number)
        return tuple(
            (jnp.where(taking, incoming, current) for incoming, current in zip(arrived, payload))
        )

    def hop_lists(payload, bit_number, taking):
        arrived = swapped((payload[0], payload[1]), "req", bit_number)
        return tuple(
            (jnp.where(taking, incoming, current) for incoming, current in zip(arrived, payload))
        )

    first_out = attend(queries[0], new_keys[:1], new_values[:1], page_table, kept[0], cache)
    group_ids = jnp.arange(moves.shape[0], dtype=jnp.int32)
    distance = jnp.max(jnp.bitwise_xor(moves, group_ids))
    moving = moves[req_index] != req_index
    bit_total = req_count.bit_length() - 1
    payload = (cache[0], queries[1, 0], new_keys[:, 0], new_values[:, 0])
    int_payload = (page_table[0], kept[1, 0])
    for bit_number in range(bit_total):
        taking = jnp.right_shift(distance, bit_number) & 1 == 1
        payload = hop_slot(payload, bit_number, taking)
        int_payload = hop_lists(int_payload, bit_number, taking)
    moved_cache = cache.at[0].set(jnp.where(moving, payload[0], cache[0]))
    second_queries = queries[1].at[0].set(jnp.where(moving, payload[1], queries[1, 0]))
    moved_keys = new_keys.at[:, 0].set(jnp.where(moving, payload[2], new_keys[:, 0]))
    moved_values = new_values.at[:, 0].set(jnp.where(moving, payload[3], new_values[:, 0]))
    moved_table = page_table.at[0].set(jnp.where(moving, int_payload[0], page_table[0]))
    second_kept = kept[1].at[0].set(jnp.where(moving, int_payload[1], kept[1, 0]))
    second_out = attend(
        second_queries, moved_keys, moved_values, moved_table, second_kept, moved_cache
    )
    return (first_out, second_out, moved_cache)


def solution(mesh):
    in_specs = (
        P(None, "req", None),
        P(None, "req", None),
        P(None, "req", None),
        P("req", "blk", None, None),
        P("req", None),
        P(None, "req", None, None),
        P(),
    )
    out_specs = (P("req", "blk"), P("req", "blk"), P("req", "blk", None, None))
    return jax.shard_map(
        on_device, mesh=mesh, in_specs=in_specs, out_specs=out_specs, check_vma=False
    )
```

profile of v0, /device:TPU:32, one launch (start us, length us, event | category | flops | bytes accessed | tf_op | source)
XLA Modules:
  0.0 323.8 jit_solution(4185208025197587633)
XLA Ops:
  1.3 1.6 copy.153
  3.0 1.6 collective-permute-start
  5.2 1.6 collective-permute-start.18
  7.5 1.5 collective-permute-start.30
  9.7 1.9 copy.46
  11.7 2.4 gather_fusion.2
  21.2 3.0 collective-permute-start.1
  24.2 8.2 %collective-permute-done.1 = s32[64]{0:T(128)S(1)} collective-permute-done((s32[64]{0:T(128)S(1)}, s32[64]{0:T(128)S(1)}, u32[]{:S(2)}, u32[]{:S(2)}) %collective-permute-start.1) | collective-permute-done | bytes 288 | tf_op jit(solution)/shard_map/ppermute | solution.py:25
  33.2 4.3 %collective-permute-done.7 = s32[8,16]{1,0:T(8,128)S(1)} collective-permute-done((s32[8,16]{1,0:T(8,128)S(1)}, s32[8,16]{1,0:T(8,128)S(1)}, u32[]{:S(2)}, u32[]{:S(2)}) %collective-permute-start.7) | collective-permute-done | bytes 544 | tf_op jit(solution)/shard_map/ppermute | solution.py:25
  37.6 3.4 %collective-permute-done.2 = s32[64]{0:T(128)S(1)} collective-permute-done((s32[64]{0:T(128)S(1)}, s32[64]{0:T(128)S(1)}, u32[]{:S(2)}, u32[]{:S(2)}) %collective-permute-start.2) | collective-permute-done | bytes 288 | tf_op jit(solution)/shard_map/ppermute | solution.py:25
  41.2 3.5 %collective-permute-done.8 = s32[8,16]{1,0:T(8,128)S(1)} collective-permute-done((s32[8,16]{1,0:T(8,128)S(1)}, s32[8,16]{1,0:T(8,128)S(1)}, u32[]{:S(2)}, u32[]{:S(2)}) %collective-permute-start.8) | collective-permute-done | bytes 544 | tf_op jit(solution)/shard_map/ppermute | solution.py:25
  44.7 3.3 %collective-permute-start.3 = (s32[64]{0:T(128)S(1)}, s32[64]{0:T(128)S(1)}, u32[]{:S(2)}, u32[]{:S(2)}) collective-permute-start(s32[64]{0:T(128)S(1)} %broadcast_select_fusion.31), channel_id=1, source_target_pairs={{0,32},{4,36},{8,40},{12,44},{16,48},{20,52},{24,56},{28,60},{32,0... | collective-permute-start | bytes 776 | tf_op jit(solution)/shard_map/ppermute | solution.py:25
  47.9 1.5 collective-permute-done.3
  49.4 2.9 collective-permute-start.9
  52.4 1.6 collective-permute-done.9
  54.0 5.9 %collective-permute-start.4 = (s32[64]{0:T(128)S(1)}, s32[64]{0:T(128)S(1)}, u32[]{:S(2)}, u32[]{:S(2)}) collective-permute-start(s32[64]{0:T(128)S(1)} %broadcast_select_fusion.32), channel_id=1, source_target_pairs={{0,64},{4,68},{8,72},{12,76},{16,80},{20,84},{24,88},{28,92},{32,9... | collective-permute-start | bytes 776 | tf_op jit(solution)/shard_map/ppermute | solution.py:25
  59.9 1.5 collective-permute-done.4
  61.4 5.9 %collective-permute-start.10 = (s32[8,16]{1,0:T(8,128)S(1)}, s32[8,16]{1,0:T(8,128)S(1)}, u32[]{:S(2)}, u32[]{:S(2)}) collective-permute-start(s32[8,16]{1,0:T(8,128)S(1)} %broadcast_select_fusion.27), channel_id=1, source_target_pairs={{0,64},{4,68},{8,72},{12,76},{16,80},{20,84},{24,88},{28,92},{32,9... | collective-permute-start | bytes 1544 | tf_op jit(solution)/shard_map/ppermute | solution.py:25
  67.3 1.6 collective-permute-done.10
  68.9 3.2 collective-permute-start.5
  72.1 1.8 collective-permute-done.5
  74.0 3.2 collective-permute-start.11
  77.4 1.7 collective-permute-done.11
  79.2 2.4 gather_fusion.3
  82.9 3.6 %gather_fusion = bf16[128,16,2,128]{3,1,2,0:T(8,128)(2,1)} fusion(bf16[2,16,16,2,8,128]{5,2,4,3,1,0:T(8,128)(2,1)} %copy.46, s32[128]{0:T(128)S(1)} %reshape.508), kind=kCustom, calls=%fused_computation | custom fusion | bytes 2098688 | tf_op jit(solution)/shard_map/gather | solution.py:58
  86.5 2.5 fusion.86
  90.7 5.2 %all-gather = bf16[8,8,8]{2,1,0:T(8,128)(2,1)S(1)} all-gather(bf16[2,8,8]{2,1,0:T(8,128)(2,1)S(1)} %convert_element_type.206), channel_id=2, replica_groups=mesh['req'=64,'blk'=4] {'blk'}, dimensions={0}, use_global_device_ids=true | all-gather | bytes 1280 | tf_op jit(solution)/shard_map/all_gather | solution.py:11
  96.1 5.2 %all-gather.1 = bf16[8,8,8]{2,1,0:T(8,128)(2,1)S(1)} all-gather(bf16[2,8,8]{2,1,0:T(8,128)(2,1)S(1)} %fusion.17), channel_id=3, replica_groups=mesh['req'=64,'blk'=4] {'blk'}, dimensions={0}, use_global_device_ids=true | all-gather | bytes 1280 | tf_op jit(solution)/shard_map/all_gather | solution.py:11
  102.6 5.4 %all-gather.2 = bf16[8,8,8,128]{3,2,1,0:T(8,128)(2,1)S(1)} all-gather(bf16[2,8,8,128]{3,2,1,0:T(8,128)(2,1)S(1)} %convolution_convert_fusion.1), channel_id=4, replica_groups=mesh['req'=64,'blk'=4] {'blk'}, dimensions={0}, use_global_device_ids=true | all-gather | bytes 163840 | tf_op jit(solution)/shard_map/all_gather | solution.py:11
  112.5 24.4 %collective-permute-done.19 = bf16[16,16,2048]{2,1,0:T(8,128)(2,1)} collective-permute-done((bf16[16,16,2048]{2,1,0:T(8,128)(2,1)}, bf16[16,16,2048]{2,1,0:T(8,128)(2,1)}, u32[]{:S(2)}, u32[]{:S(2)}) %collective-permute-start.19) | collective-permute-done | bytes 1048608 | tf_op jit(solution)/shard_map/ppermute | solution.py:25
  140.2 2.8 collective-permute-start.25
  146.8 16.3 %collective-permute-done.32 = bf16[2,1024]{1,0:T(2,128)(2,1)S(1)} collective-permute-done((bf16[2,1024]{1,0:T(2,128)(2,1)S(1)}, bf16[2,1024]{1,0:T(2,128)(2,1)S(1)}, u32[]{:S(2)}, u32[]{:S(2)}) %collective-permute-start.32) | collective-permute-done | bytes 4128 | tf_op jit(solution)/shard_map/ppermute | solution.py:25
  163.1 3.0 collective-permute-start.33
  166.3 3.0 collective-permute-start.27
  170.2 4.6 %collective-permute-start.34 = (bf16[2,1024]{1,0:T(2,128)(2,1)S(1)}, bf16[2,1024]{1,0:T(2,128)(2,1)S(1)}, u32[]{:S(2)}, u32[]{:S(2)}) collective-permute-start(bf16[2,1024]{1,0:T(2,128)(2,1)S(1)} %broadcast_select_fusion.16), channel_id=1, source_target_pairs={{0,64},{4,68},{8,72},{12,76},{16,80},{20,84},{24,88},{28,92},{32,9... | collective-permute-start | bytes 12296 | tf_op jit(solution)/shard_map/ppermute | solution.py:25
  174.8 35.6 %collective-permute-done.27 = bf16[2,1024]{1,0:T(2,128)(2,1)S(1)} collective-permute-done((bf16[2,1024]{1,0:T(2,128)(2,1)S(1)}, bf16[2,1024]{1,0:T(2,128)(2,1)S(1)}, u32[]{:S(2)}, u32[]{:S(2)}) %collective-permute-start.27) | collective-permute-done | bytes 4128 | tf_op jit(solution)/shard_map/ppermute | solution.py:25
  210.4 5.7 %collective-permute-start.28 = (bf16[2,1024]{1,0:T(2,128)(2,1)S(1)}, bf16[2,1024]{1,0:T(2,128)(2,1)S(1)}, u32[]{:S(2)}, u32[]{:S(2)}) collective-permute-start(bf16[2,1024]{1,0:T(2,128)(2,1)S(1)} %broadcast_select_fusion.17), channel_id=1, source_target_pairs={{0,64},{4,68},{8,72},{12,76},{16,80},{20,84},{24,88},{28,92},{32,9... | collective-permute-start | bytes 12296 | tf_op jit(solution)/shard_map/ppermute | solution.py:25
  216.1 3.3 %collective-permute-start.35 = (bf16[2,1024]{1,0:T(2,128)(2,1)S(1)}, bf16[2,1024]{1,0:T(2,128)(2,1)S(1)}, u32[]{:S(2)}, u32[]{:S(2)}) collective-permute-start(bf16[2,1024]{1,0:T(2,128)(2,1)S(1)} %broadcast_select_fusion.18), channel_id=1, source_target_pairs={{0,128},{4,132},{8,136},{12,140},{16,144},{20,148},{24,152},{28,15... | collective-permute-start | bytes 12296 | tf_op jit(solution)/shard_map/ppermute | solution.py:25
  219.9 3.9 %collective-permute-start.14 = (bf16[8192]{0:T(1024)(128)(2,1)S(1)}, bf16[8192]{0:T(1024)(128)(2,1)S(1)}, u32[]{:S(2)}, u32[]{:S(2)}) collective-permute-start(bf16[8192]{0:T(1024)(128)(2,1)S(1)} %broadcast_select_fusion.6), channel_id=1, source_target_pairs={{0,16},{4,20},{8,24},{12,28},{16,0},{20,4},{24,8},{28,12},{32,48},... | collective-permute-start | bytes 49160 | tf_op jit(solution)/shard_map/ppermute | solution.py:25
  224.2 44.0 %collective-permute-done.14 = bf16[8192]{0:T(1024)(128)(2,1)S(1)} collective-permute-done((bf16[8192]{0:T(1024)(128)(2,1)S(1)}, bf16[8192]{0:T(1024)(128)(2,1)S(1)}, u32[]{:S(2)}, u32[]{:S(2)}) %collective-permute-start.14) | collective-permute-done | bytes 16416 | tf_op jit(solution)/shard_map/ppermute | solution.py:25
  268.3 4.6 %collective-permute-done.15 = bf16[8192]{0:T(1024)(128)(2,1)S(1)} collective-permute-done((bf16[8192]{0:T(1024)(128)(2,1)S(1)}, bf16[8192]{0:T(1024)(128)(2,1)S(1)}, u32[]{:S(2)}, u32[]{:S(2)}) %collective-permute-start.15) | collective-permute-done | bytes 16416 | tf_op jit(solution)/shard_map/ppermute | solution.py:25
  272.9 2.6 collective-permute-start.16
  277.2 3.4 %collective-permute-done.16 = bf16[8192]{0:T(1024)(128)(2,1)S(1)} collective-permute-done((bf16[8192]{0:T(1024)(128)(2,1)S(1)}, bf16[8192]{0:T(1024)(128)(2,1)S(1)}, u32[]{:S(2)}, u32[]{:S(2)}) %collective-permute-start.16) | collective-permute-done | bytes 16416 | tf_op jit(solution)/shard_map/ppermute | solution.py:25
  281.0 19.2 %collective-permute-done.17 = bf16[8192]{0:T(1024)(128)(2,1)S(1)} collective-permute-done((bf16[8192]{0:T(1024)(128)(2,1)S(1)}, bf16[8192]{0:T(1024)(128)(2,1)S(1)}, u32[]{:S(2)}, u32[]{:S(2)}) %collective-permute-start.17) | collective-permute-done | bytes 16416 | tf_op jit(solution)/shard_map/ppermute | solution.py:25
  300.6 1.8 bitcast_dynamic-update-slice_fusion
  306.1 5.2 %all-gather.3 = bf16[8,8,8]{2,1,0:T(8,128)(2,1)S(1)} all-gather(bf16[2,8,8]{2,1,0:T(8,128)(2,1)S(1)} %convert_element_type.221), channel_id=5, replica_groups=mesh['req'=64,'blk'=4] {'blk'}, dimensions={0}, use_global_device_ids=true | all-gather | bytes 1280 | tf_op jit(solution)/shard_map/all_gather | solution.py:11
  311.5 5.2 %all-gather.4 = bf16[8,8,8]{2,1,0:T(8,128)(2,1)S(1)} all-gather(bf16[2,8,8]{2,1,0:T(8,128)(2,1)S(1)} %fusion.19), channel_id=6, replica_groups=mesh['req'=64,'blk'=4] {'blk'}, dimensions={0}, use_global_device_ids=true | all-gather | bytes 1280 | tf_op jit(solution)/shard_map/all_gather | solution.py:11
  317.0 5.4 %all-gather.5 = bf16[8,8,8,128]{3,2,1,0:T(8,128)(2,1)S(1)} all-gather(bf16[2,8,8,128]{3,2,1,0:T(8,128)(2,1)S(1)} %convolution_convert_fusion), channel_id=7, replica_groups=mesh['req'=64,'blk'=4] {'blk'}, dimensions={0}, use_global_device_ids=true | all-gather | bytes 163840 | tf_op jit(solution)/shard_map/all_gather | solution.py:11
  (183 shorter events, 33.2 us)
Async XLA Ops:
  1.3 1.6 copy-start.3
  1.3 1.6 copy-start.4
  1.3 3.3 %copy-start.2 = (s32[2,2,8,16]{3,2,1,0:T(8,128)S(1)}, s32[2,2,8,16]{3,2,1,0:T(8,128)}, u32[]{:S(2)}) copy-start(s32[2,2,8,16]{3,2,1,0:T(8,128)} %param.28) | copy-start | bytes 6148
  2.9 3.9 %copy-start.1 = (bf16[2,2,8192]{2,1,0:T(2,128)(2,1)S(1)}, bf16[2,2,8192]{2,1,0:T(2,128)(2,1)}, u32[]{:S(2)}) copy-start(bf16[2,2,8192]{2,1,0:T(2,128)(2,1)} %param.23) | copy-start | bytes 196612
  3.0 17.6 %collective-permute-start = (s32[64]{0:T(128)S(1)}, s32[64]{0:T(128)S(1)}, u32[]{:S(2)}, u32[]{:S(2)}) collective-permute-start(s32[64]{0:T(128)S(1)} %slice_bitcast_fusion.4), channel_id=1, source_target_pairs={{0,4},{4,0},{8,12},{12,8},{16,20},{20,16},{24,28},{28,24},{32,36},... | collective-permute-start | bytes 776 | tf_op jit(solution)/shard_map/ppermute | solution.py:25
  4.6 16.6 %collective-permute-start.6 = (s32[8,16]{1,0:T(8,128)S(1)}, s32[8,16]{1,0:T(8,128)S(1)}, u32[]{:S(2)}, u32[]{:S(2)}) collective-permute-start(s32[8,16]{1,0:T(8,128)S(1)} %slice_bitcast_fusion.3), channel_id=1, source_target_pairs={{0,4},{4,0},{8,12},{12,8},{16,20},{20,16},{24,28},{28,24},{32,36},... | collective-permute-start | bytes 1544 | tf_op jit(solution)/shard_map/ppermute | solution.py:25
  5.2 103.3 %collective-permute-start.18 = (bf16[16,16,2048]{2,1,0:T(8,128)(2,1)S(1)}, bf16[16,16,2048]{2,1,0:T(8,128)(2,1)}, u32[]{:S(2)}, u32[]{:S(2)}) collective-permute-start(bf16[16,16,2048]{2,1,0:T(8,128)(2,1)S(1)} %slice_bitcast_fusion), channel_id=1, source_target_pairs={{0,4},{4,0},{8,12},{12,8},{16,20},{20,16},{24,28},{28,24},{32,36},... | collective-permute-start | bytes 3145736 | tf_op jit(solution)/shard_map/ppermute | solution.py:25
  6.9 162.4 %collective-permute-start.12 = (bf16[8192]{0:T(1024)(128)(2,1)S(1)}, bf16[8192]{0:T(1024)(128)(2,1)S(1)}, u32[]{:S(2)}, u32[]{:S(2)}) collective-permute-start(bf16[8192]{0:T(1024)(128)(2,1)S(1)} %slice_reduce_fusion), channel_id=1, source_target_pairs={{0,4},{4,0},{8,12},{12,8},{16,20},{20,16},{24,28},{28,24},{32,36},... | collective-permute-start | bytes 49160 | tf_op jit(solution)/shard_map/ppermute | solution.py:25
  7.5 131.8 %collective-permute-start.30 = (bf16[2,1024]{1,0:T(2,128)(2,1)S(1)}, bf16[2,1024]{1,0:T(2,128)(2,1)S(1)}, u32[]{:S(2)}, u32[]{:S(2)}) collective-permute-start(bf16[2,1024]{1,0:T(2,128)(2,1)S(1)} %bitcast.216), channel_id=1, source_target_pairs={{0,4},{4,0},{8,12},{12,8},{16,20},{20,16},{24,28},{28,24},{32,36},... | collective-permute-start | bytes 12296 | tf_op jit(solution)/shard_map/ppermute | solution.py:25
  11.7 2.5 copy-start.5
  20.6 119.7 %collective-permute-start.24 = (bf16[2,1024]{1,0:T(2,128)(2,1)S(1)}, bf16[2,1024]{1,0:T(2,128)(2,1)S(1)}, u32[]{:S(2)}, u32[]{:S(2)}) collective-permute-start(bf16[2,1024]{1,0:T(2,128)(2,1)S(1)} %bitcast.217), channel_id=1, source_target_pairs={{0,4},{4,0},{8,12},{12,8},{16,20},{20,16},{24,28},{28,24},{32,36},... | collective-permute-start | bytes 12296 | tf_op jit(solution)/shard_map/ppermute | solution.py:25
  21.2 11.2 %collective-permute-start.1 = (s32[64]{0:T(128)S(1)}, s32[64]{0:T(128)S(1)}, u32[]{:S(2)}, u32[]{:S(2)}) collective-permute-start(s32[64]{0:T(128)S(1)} %broadcast_select_fusion.29), channel_id=1, source_target_pairs={{0,8},{4,12},{8,0},{12,4},{16,24},{20,28},{24,16},{28,20},{32,40},... | collective-permute-start | bytes 776 | tf_op jit(solution)/shard_map/ppermute | solution.py:25
  32.4 5.1 %collective-permute-start.7 = (s32[8,16]{1,0:T(8,128)S(1)}, s32[8,16]{1,0:T(8,128)S(1)}, u32[]{:S(2)}, u32[]{:S(2)}) collective-permute-start(s32[8,16]{1,0:T(8,128)S(1)} %broadcast_select_fusion.24), channel_id=1, source_target_pairs={{0,8},{4,12},{8,0},{12,4},{16,24},{20,28},{24,16},{28,20},{32,40},... | collective-permute-start | bytes 1544 | tf_op jit(solution)/shard_map/ppermute | solution.py:25
  37.5 3.5 %collective-permute-start.2 = (s32[64]{0:T(128)S(1)}, s32[64]{0:T(128)S(1)}, u32[]{:S(2)}, u32[]{:S(2)}) collective-permute-start(s32[64]{0:T(128)S(1)} %broadcast_select_fusion.30), channel_id=1, source_target_pairs={{0,16},{4,20},{8,24},{12,28},{16,0},{20,4},{24,8},{28,12},{32,48},... | collective-permute-start | bytes 776 | tf_op jit(solution)/shard_map/ppermute | solution.py:25
  41.0 3.6 %collective-permute-start.8 = (s32[8,16]{1,0:T(8,128)S(1)}, s32[8,16]{1,0:T(8,128)S(1)}, u32[]{:S(2)}, u32[]{:S(2)}) collective-permute-start(s32[8,16]{1,0:T(8,128)S(1)} %broadcast_select_fusion.25), channel_id=1, source_target_pairs={{0,16},{4,20},{8,24},{12,28},{16,0},{20,4},{24,8},{28,12},{32,48},... | collective-permute-start | bytes 1544 | tf_op jit(solution)/shard_map/ppermute | solution.py:25
  44.7 4.8 %collective-permute-start.3 = (s32[64]{0:T(128)S(1)}, s32[64]{0:T(128)S(1)}, u32[]{:S(2)}, u32[]{:S(2)}) collective-permute-start(s32[64]{0:T(128)S(1)} %broadcast_select_fusion.31), channel_id=1, source_target_pairs={{0,32},{4,36},{8,40},{12,44},{16,48},{20,52},{24,56},{28,60},{32,0... | collective-permute-start | bytes 776 | tf_op jit(solution)/shard_map/ppermute | solution.py:25
  49.4 4.5 %collective-permute-start.9 = (s32[8,16]{1,0:T(8,128)S(1)}, s32[8,16]{1,0:T(8,128)S(1)}, u32[]{:S(2)}, u32[]{:S(2)}) collective-permute-start(s32[8,16]{1,0:T(8,128)S(1)} %broadcast_select_fusion.26), channel_id=1, source_target_pairs={{0,32},{4,36},{8,40},{12,44},{16,48},{20,52},{24,56},{28,60},{32,0... | collective-permute-start | bytes 1544 | tf_op jit(solution)/shard_map/ppermute | solution.py:25
  54.0 7.5 %collective-permute-start.4 = (s32[64]{0:T(128)S(1)}, s32[64]{0:T(128)S(1)}, u32[]{:S(2)}, u32[]{:S(2)}) collective-permute-start(s32[64]{0:T(128)S(1)} %broadcast_select_fusion.32), channel_id=1, source_target_pairs={{0,64},{4,68},{8,72},{12,76},{16,80},{20,84},{24,88},{28,92},{32,9... | collective-permute-start | bytes 776 | tf_op jit(solution)/shard_map/ppermute | solution.py:25
  61.4 7.5 %collective-permute-start.10 = (s32[8,16]{1,0:T(8,128)S(1)}, s32[8,16]{1,0:T(8,128)S(1)}, u32[]{:S(2)}, u32[]{:S(2)}) collective-permute-start(s32[8,16]{1,0:T(8,128)S(1)} %broadcast_select_fusion.27), channel_id=1, source_target_pairs={{0,64},{4,68},{8,72},{12,76},{16,80},{20,84},{24,88},{28,92},{32,9... | collective-permute-start | bytes 1544 | tf_op jit(solution)/shard_map/ppermute | solution.py:25
  68.9 5.0 %collective-permute-start.5 = (s32[64]{0:T(128)S(1)}, s32[64]{0:T(128)S(1)}, u32[]{:S(2)}, u32[]{:S(2)}) collective-permute-start(s32[64]{0:T(128)S(1)} %broadcast_select_fusion.33), channel_id=1, source_target_pairs={{0,128},{4,132},{8,136},{12,140},{16,144},{20,148},{24,152},{28,15... | collective-permute-start | bytes 776 | tf_op jit(solution)/shard_map/ppermute | solution.py:25
  74.0 5.1 %collective-permute-start.11 = (s32[8,16]{1,0:T(8,128)S(1)}, s32[8,16]{1,0:T(8,128)S(1)}, u32[]{:S(2)}, u32[]{:S(2)}) collective-permute-start(s32[8,16]{1,0:T(8,128)S(1)} %broadcast_select_fusion.28), channel_id=1, source_target_pairs={{0,128},{4,132},{8,136},{12,140},{16,144},{20,148},{24,152},{28,15... | collective-permute-start | bytes 1544 | tf_op jit(solution)/shard_map/ppermute | solution.py:25
  109.6 27.3 %collective-permute-start.19 = (bf16[16,16,2048]{2,1,0:T(8,128)(2,1)}, bf16[16,16,2048]{2,1,0:T(8,128)(2,1)}, u32[]{:S(2)}, u32[]{:S(2)}) collective-permute-start(bf16[16,16,2048]{2,1,0:T(8,128)(2,1)} %broadcast_select_fusion), channel_id=1, source_target_pairs={{0,8},{4,12},{8,0},{12,4},{16,24},{20,28},{24,16},{28,20},{32,40},... | collective-permute-start | bytes 3145736 | tf_op jit(solution)/shard_map/ppermute | solution.py:25
  138.2 27.8 %collective-permute-start.20 = (bf16[16,16,2048]{2,1,0:T(8,128)(2,1)S(1)}, bf16[16,16,2048]{2,1,0:T(8,128)(2,1)S(1)}, u32[]{:S(2)}, u32[]{:S(2)}) collective-permute-start(bf16[16,16,2048]{2,1,0:T(8,128)(2,1)S(1)} %broadcast_select_fusion.1), channel_id=1, source_target_pairs={{0,16},{4,20},{8,24},{12,28},{16,0},{20,4},{24,8},{28,12},{32,48},... | collective-permute-start | bytes 3145736 | tf_op jit(solution)/shard_map/ppermute | solution.py:25
  139.3 5.2 %collective-permute-start.31 = (bf16[2,1024]{1,0:T(2,128)(2,1)S(1)}, bf16[2,1024]{1,0:T(2,128)(2,1)S(1)}, u32[]{:S(2)}, u32[]{:S(2)}) collective-permute-start(bf16[2,1024]{1,0:T(2,128)(2,1)S(1)} %broadcast_select_fusion.10), channel_id=1, source_target_pairs={{0,8},{4,12},{8,0},{12,4},{16,24},{20,28},{24,16},{28,20},{32,40},... | collective-permute-start | bytes 12296 | tf_op jit(solution)/shard_map/ppermute | solution.py:25
  140.2 5.4 %collective-permute-start.25 = (bf16[2,1024]{1,0:T(2,128)(2,1)S(1)}, bf16[2,1024]{1,0:T(2,128)(2,1)S(1)}, u32[]{:S(2)}, u32[]{:S(2)}) collective-permute-start(bf16[2,1024]{1,0:T(2,128)(2,1)S(1)} %broadcast_select_fusion.11), channel_id=1, source_target_pairs={{0,8},{4,12},{8,0},{12,4},{16,24},{20,28},{24,16},{28,20},{32,40},... | collective-permute-start | bytes 12296 | tf_op jit(solution)/shard_map/ppermute | solution.py:25
  144.5 18.5 %collective-permute-start.32 = (bf16[2,1024]{1,0:T(2,128)(2,1)S(1)}, bf16[2,1024]{1,0:T(2,128)(2,1)S(1)}, u32[]{:S(2)}, u32[]{:S(2)}) collective-permute-start(bf16[2,1024]{1,0:T(2,128)(2,1)S(1)} %broadcast_select_fusion.12), channel_id=1, source_target_pairs={{0,16},{4,20},{8,24},{12,28},{16,0},{20,4},{24,8},{28,12},{32,48},... | collective-permute-start | bytes 12296 | tf_op jit(solution)/shard_map/ppermute | solution.py:25
  145.7 20.6 %collective-permute-start.26 = (bf16[2,1024]{1,0:T(2,128)(2,1)S(1)}, bf16[2,1024]{1,0:T(2,128)(2,1)S(1)}, u32[]{:S(2)}, u32[]{:S(2)}) collective-permute-start(bf16[2,1024]{1,0:T(2,128)(2,1)S(1)} %broadcast_select_fusion.13), channel_id=1, source_target_pairs={{0,16},{4,20},{8,24},{12,28},{16,0},{20,4},{24,8},{28,12},{32,48},... | collective-permute-start | bytes 12296 | tf_op jit(solution)/shard_map/ppermute | solution.py:25
  163.1 7.1 %collective-permute-start.33 = (bf16[2,1024]{1,0:T(2,128)(2,1)S(1)}, bf16[2,1024]{1,0:T(2,128)(2,1)S(1)}, u32[]{:S(2)}, u32[]{:S(2)}) collective-permute-start(bf16[2,1024]{1,0:T(2,128)(2,1)S(1)} %broadcast_select_fusion.14), channel_id=1, source_target_pairs={{0,32},{4,36},{8,40},{12,44},{16,48},{20,52},{24,56},{28,60},{32,0... | collective-permute-start | bytes 12296 | tf_op jit(solution)/shard_map/ppermute | solution.py:25
  166.2 53.2 %collective-permute-start.21 = (bf16[16,16,2048]{2,1,0:T(8,128)(2,1)S(1)}, bf16[16,16,2048]{2,1,0:T(8,128)(2,1)S(1)}, u32[]{:S(2)}, u32[]{:S(2)}) collective-permute-start(bf16[16,16,2048]{2,1,0:T(8,128)(2,1)S(1)} %broadcast_select_fusion.2), channel_id=1, source_target_pairs={{0,32},{4,36},{8,40},{12,44},{16,48},{20,52},{24,56},{28,60},{32,0... | collective-permute-start | bytes 3145736 | tf_op jit(solution)/shard_map/ppermute | solution.py:25
  166.3 44.1 %collective-permute-start.27 = (bf16[2,1024]{1,0:T(2,128)(2,1)S(1)}, bf16[2,1024]{1,0:T(2,128)(2,1)S(1)}, u32[]{:S(2)}, u32[]{:S(2)}) collective-permute-start(bf16[2,1024]{1,0:T(2,128)(2,1)S(1)} %broadcast_select_fusion.15), channel_id=1, source_target_pairs={{0,32},{4,36},{8,40},{12,44},{16,48},{20,52},{24,56},{28,60},{32,0... | collective-permute-start | bytes 12296 | tf_op jit(solution)/shard_map/ppermute | solution.py:25
  169.3 50.6 %collective-permute-start.13 = (bf16[8192]{0:T(1024)(128)(2,1)S(1)}, bf16[8192]{0:T(1024)(128)(2,1)S(1)}, u32[]{:S(2)}, u32[]{:S(2)}) collective-permute-start(bf16[8192]{0:T(1024)(128)(2,1)S(1)} %broadcast_select_fusion.5), channel_id=1, source_target_pairs={{0,8},{4,12},{8,0},{12,4},{16,24},{20,28},{24,16},{28,20},{32,40},... | collective-permute-start | bytes 49160 | tf_op jit(solution)/shard_map/ppermute | solution.py:25
  170.2 45.9 %collective-permute-start.34 = (bf16[2,1024]{1,0:T(2,128)(2,1)S(1)}, bf16[2,1024]{1,0:T(2,128)(2,1)S(1)}, u32[]{:S(2)}, u32[]{:S(2)}) collective-permute-start(bf16[2,1024]{1,0:T(2,128)(2,1)S(1)} %broadcast_select_fusion.16), channel_id=1, source_target_pairs={{0,64},{4,68},{8,72},{12,76},{16,80},{20,84},{24,88},{28,92},{32,9... | collective-permute-start | bytes 12296 | tf_op jit(solution)/shard_map/ppermute | solution.py:25
  210.4 13.4 %collective-permute-start.28 = (bf16[2,1024]{1,0:T(2,128)(2,1)S(1)}, bf16[2,1024]{1,0:T(2,128)(2,1)S(1)}, u32[]{:S(2)}, u32[]{:S(2)}) collective-permute-start(bf16[2,1024]{1,0:T(2,128)(2,1)S(1)} %broadcast_select_fusion.17), channel_id=1, source_target_pairs={{0,64},{4,68},{8,72},{12,76},{16,80},{20,84},{24,88},{28,92},{32,9... | collective-permute-start | bytes 12296 | tf_op jit(solution)/shard_map/ppermute | solution.py:25
  216.1 52.1 %collective-permute-start.35 = (bf16[2,1024]{1,0:T(2,128)(2,1)S(1)}, bf16[2,1024]{1,0:T(2,128)(2,1)S(1)}, u32[]{:S(2)}, u32[]{:S(2)}) collective-permute-start(bf16[2,1024]{1,0:T(2,128)(2,1)S(1)} %broadcast_select_fusion.18), channel_id=1, source_target_pairs={{0,128},{4,132},{8,136},{12,140},{16,144},{20,148},{24,152},{28,15... | collective-permute-start | bytes 12296 | tf_op jit(solution)/shard_map/ppermute | solution.py:25
  219.5 56.0 %collective-permute-start.22 = (bf16[16,16,2048]{2,1,0:T(8,128)(2,1)S(1)}, bf16[16,16,2048]{2,1,0:T(8,128)(2,1)S(1)}, u32[]{:S(2)}, u32[]{:S(2)}) collective-permute-start(bf16[16,16,2048]{2,1,0:T(8,128)(2,1)S(1)} %broadcast_select_fusion.3), channel_id=1, source_target_pairs={{0,64},{4,68},{8,72},{12,76},{16,80},{20,84},{24,88},{28,92},{32,9... | collective-permute-start | bytes 3145736 | tf_op jit(solution)/shard_map/ppermute | solution.py:25
  219.9 48.3 %collective-permute-start.14 = (bf16[8192]{0:T(1024)(128)(2,1)S(1)}, bf16[8192]{0:T(1024)(128)(2,1)S(1)}, u32[]{:S(2)}, u32[]{:S(2)}) collective-permute-start(bf16[8192]{0:T(1024)(128)(2,1)S(1)} %broadcast_select_fusion.6), channel_id=1, source_target_pairs={{0,16},{4,20},{8,24},{12,28},{16,0},{20,4},{24,8},{28,12},{32,48},... | collective-permute-start | bytes 49160 | tf_op jit(solution)/shard_map/ppermute | solution.py:25
  223.8 53.2 %collective-permute-start.29 = (bf16[2,1024]{1,0:T(2,128)(2,1)S(1)}, bf16[2,1024]{1,0:T(2,128)(2,1)S(1)}, u32[]{:S(2)}, u32[]{:S(2)}) collective-permute-start(bf16[2,1024]{1,0:T(2,128)(2,1)S(1)} %broadcast_select_fusion.19), channel_id=1, source_target_pairs={{0,128},{4,132},{8,136},{12,140},{16,144},{20,148},{24,152},{28,15... | collective-permute-start | bytes 12296 | tf_op jit(solution)/shard_map/ppermute | solution.py:25
  268.3 4.6 %collective-permute-start.15 = (bf16[8192]{0:T(1024)(128)(2,1)S(1)}, bf16[8192]{0:T(1024)(128)(2,1)S(1)}, u32[]{:S(2)}, u32[]{:S(2)}) collective-permute-start(bf16[8192]{0:T(1024)(128)(2,1)S(1)} %broadcast_select_fusion.7), channel_id=1, source_target_pairs={{0,32},{4,36},{8,40},{12,44},{16,48},{20,52},{24,56},{28,60},{32,0... | collective-permute-start | bytes 49160 | tf_op jit(solution)/shard_map/ppermute | solution.py:25
  272.9 7.6 %collective-permute-start.16 = (bf16[8192]{0:T(1024)(128)(2,1)S(1)}, bf16[8192]{0:T(1024)(128)(2,1)S(1)}, u32[]{:S(2)}, u32[]{:S(2)}) collective-permute-start(bf16[8192]{0:T(1024)(128)(2,1)S(1)} %broadcast_select_fusion.8), channel_id=1, source_target_pairs={{0,64},{4,68},{8,72},{12,76},{16,80},{20,84},{24,88},{28,92},{32,9... | collective-permute-start | bytes 49160 | tf_op jit(solution)/shard_map/ppermute | solution.py:25
  276.6 24.0 %collective-permute-start.23 = (bf16[16,16,2048]{2,1,0:T(8,128)(2,1)}, bf16[16,16,2048]{2,1,0:T(8,128)(2,1)}, u32[]{:S(2)}, u32[]{:S(2)}) collective-permute-start(bf16[16,16,2048]{2,1,0:T(8,128)(2,1)} %broadcast_select_fusion.4), channel_id=1, source_target_pairs={{0,128},{4,132},{8,136},{12,140},{16,144},{20,148},{24,152},{28,15... | collective-permute-start | bytes 3145736 | tf_op jit(solution)/shard_map/ppermute | solution.py:25
  280.6 19.6 %collective-permute-start.17 = (bf16[8192]{0:T(1024)(128)(2,1)S(1)}, bf16[8192]{0:T(1024)(128)(2,1)S(1)}, u32[]{:S(2)}, u32[]{:S(2)}) collective-permute-start(bf16[8192]{0:T(1024)(128)(2,1)S(1)} %broadcast_select_fusion.9), channel_id=1, source_target_pairs={{0,128},{4,132},{8,136},{12,140},{16,144},{20,148},{24,152},{28,15... | collective-permute-start | bytes 49160 | tf_op jit(solution)/shard_map/ppermute | solution.py:25
  302.4 1.3 copy-start
where the time goes:
time: 327 us; the launch traced here: 324 us
  waiting for transfers between devices  178 us (54%)
  starting transfers between devices  71.4 us (22%)
  blocking collectives  31.6 us (10%)
  local copies, waits for them, and re-layouts  22.6 us (7%)
  other arithmetic  10 us (3%)
  between operations  5.92 us (2%)
  matrix products  4.03 us (1%)
    ppermute x36, waiting for transfers between devices, swapped(): lax.ppermute(array, axis, [(i, i ^ 1 << distance) for i in range(lax.axis...  178 us
    ppermute x36, starting transfers between devices, swapped(): lax.ppermute(array, axis, [(i, i ^ 1 << distance) for i in range(lax.axis...  71.4 us
    all_gather x6, blocking collectives, joined(): lax.all_gather(part.astype(kind), axis)  31.6 us
  transfers between devices with their start and end apart: 36, of which 18 were waited for; matrix products, arithmetic and copies ran while one was open for 8% of the time, Pallas kernels for 0%

commit v1 on v0

v1 whole, which is shorter than its diff:
```python
import functools

import jax
import jax.numpy as jnp
from jax import lax
from jax.experimental import pallas as pl
from jax.experimental.pallas import tpu as pltpu
from jax.sharding import PartitionSpec as P

NEG = -1e30
MESH = pl.DeviceIdType.MESH


def partner_of(index, distance, bits):
    other = 0
    for bit in range(bits):
        value = (index // (1 << bit)) % 2
        if (distance >> bit) & 1:
            value = 1 - value
        other = other + value * (1 << bit)
    return other


def move_kernel(distance, bits, rows_ref, out_ref, got_rows, got_out, send, recv):
    g = lax.axis_index("req")
    there = {"req": partner_of(g, distance, bits)}
    barrier = pltpu.get_barrier_semaphore()
    pl.semaphore_signal(barrier, inc=1, device_id=there, device_id_type=MESH)
    pl.semaphore_wait(barrier, 1)
    copies = [
        pltpu.make_async_remote_copy(
            src_ref=rows_ref.at[0],
            dst_ref=got_rows,
            send_sem=send.at[0],
            recv_sem=recv.at[0],
            device_id=there,
            device_id_type=MESH,
        ),
        pltpu.make_async_remote_copy(
            src_ref=out_ref,
            dst_ref=got_out,
            send_sem=send.at[1],
            recv_sem=recv.at[1],
            device_id=there,
            device_id_type=MESH,
        ),
    ]
    for copy in copies:
        copy.start()
    for copy in copies:
        copy.wait()


def move(distance, bits, cache, row):
    return pl.pallas_call(
        functools.partial(move_kernel, distance, bits),
        out_shape=(
            jax.ShapeDtypeStruct(cache.shape[1:], cache.dtype),
            jax.ShapeDtypeStruct(row.shape, row.dtype),
        ),
        in_specs=[pl.BlockSpec(memory_space=pl.ANY)] * 2,
        out_specs=(pl.BlockSpec(memory_space=pl.ANY),) * 2,
        scratch_shapes=[pltpu.SemaphoreType.DMA((2,)), pltpu.SemaphoreType.DMA((2,))],
        compiler_params=pltpu.CompilerParams(collective_id=distance, has_side_effects=True),
    )(cache, row)


def partials(queries, cache, table, kept, first_page):
    steps, rows, heads = kept.shape[:3]
    pages, size, width = cache.shape[1:]
    head_size = width // (2 * heads)
    stored = jax.vmap(lambda t, k: t[k], (0, 1), 1)(table, kept)
    here = first_page + jnp.arange(pages, dtype=jnp.int32)
    use = jnp.any(stored[..., None] == here, axis=3)
    view = cache.reshape(rows, pages, size, 2, heads, head_size)
    q = queries.reshape(steps, rows, heads, -1, head_size)
    scores = jnp.einsum(
        "srjgd,rptjd->srjgpt", q, view[:, :, :, 0], preferred_element_type=jnp.float32
    )
    scores = scores * head_size**-0.5
    mask = use[:, :, :, None, :, None]
    scores = jnp.where(mask, scores, NEG)
    top = jnp.max(scores, axis=(4, 5))
    weights = jnp.where(mask, jnp.exp(scores - top[..., None, None]), 0.0)
    total = jnp.sum(weights, axis=(4, 5))
    mixed = jnp.einsum(
        "srjgpt,rptjd->srjgd",
        weights.astype(jnp.bfloat16),
        view[:, :, :, 1],
        preferred_element_type=jnp.float32,
    )
    return top, total, mixed


def finish(packed, queries, keys, values, blk, own):
    head_size = packed.shape[-1] // 2
    steps, rows = queries.shape[:2]
    mixed, top, total = (
        packed[..., :head_size],
        packed[..., head_size],
        packed[..., head_size + 1],
    )
    q = lax.dynamic_slice_in_dim(
        queries.reshape(steps, rows, -1, packed.shape[4], head_size), blk * own, own, 2
    )
    k = lax.dynamic_slice_in_dim(keys.reshape(steps, rows, -1, head_size), blk * own, own, 2)
    v = lax.dynamic_slice_in_dim(values.reshape(steps, rows, -1, head_size), blk * own, own, 2)
    fresh = jnp.einsum("srjgd,nrjd->srjgn", q, k, preferred_element_type=jnp.float32)
    fresh = fresh * head_size**-0.5
    seen = jnp.arange(steps)[None, :] <= jnp.arange(steps)[:, None]
    seen = seen[:, None, None, None, :]
    fresh = jnp.where(seen, fresh, NEG)
    best = jnp.maximum(jnp.max(top, axis=0), jnp.max(fresh, axis=-1))
    scale = jnp.exp(top - best)
    weights = jnp.where(seen, jnp.exp(fresh - best[..., None]), 0.0)
    total = jnp.sum(total * scale, axis=0) + jnp.sum(weights, axis=-1)
    mixed = jnp.sum(mixed * scale[..., None], axis=0) + jnp.einsum(
        "srjgn,nrjd->srjgd",
        weights.astype(jnp.bfloat16),
        v,
        preferred_element_type=jnp.float32,
    )
    return (mixed / total[..., None]).astype(jnp.bfloat16).reshape(steps, rows, -1)


def on_device(queries, new_keys, new_values, cache, page_table, kept, moves):
    blk = lax.axis_index("blk")
    g = lax.axis_index("req")
    blks, count = lax.axis_size("blk"), lax.axis_size("req")
    bits = count.bit_length() - 1
    own = kept.shape[2] // blks
    top, total, mixed = partials(queries, cache, page_table, kept, blk * cache.shape[1])
    packed = jnp.concatenate(
        [mixed, jnp.stack([top, total] * (mixed.shape[-1] // 2), axis=-1)], axis=-1
    )
    packed = lax.all_to_all(packed, "blk", 2, 0, tiled=True)
    packed = packed.reshape(blks, -1, *packed.shape[1:])
    out = finish(packed, queries, new_keys, new_values, blk, own)
    row = out[1, 0].reshape(-1, 128)
    branches = [functools.partial(move, d, bits) for d in range(1, count)]
    got_rows, got_out = lax.switch(moves[0] - 1, branches, cache, row)
    moving = moves[g] != g
    after = jnp.stack([jnp.where(moving, got_rows, cache[0]), cache[1]])
    second = jnp.stack([jnp.where(moving, got_out.reshape(-1), out[1, 0]), out[1, 1]])
    return out[0], second, after


def solution(mesh):
    in_specs = (
        P(None, "req", None),
        P(None, "req", None),
        P(None, "req", None),
        P("req", "blk", None, None),
        P("req", None),
        P(None, "req", None, None),
        P(),
    )
    out_specs = (P("req", "blk"), P("req", "blk"), P("req", "blk", None, None))
    return jax.shard_map(
        on_device, mesh=mesh, in_specs=in_specs, out_specs=out_specs, check_vma=False
    )
```

time: 327 us -> 128 us (0.39)
  waiting for transfers between devices: 178 us -> 3.68 us
  starting transfers between devices: 71.4 us -> 3.41 us
  Pallas kernels: 0 us -> 50.1 us
  blocking collectives: 31.6 us -> 0 us
  local copies, waits for them, and re-layouts: 22.6 us -> 50.1 us
  between operations: 5.92 us -> 2.19 us
    ppermute x36 -> x0, waiting for transfers between devices: 178 us -> none  [swapped(): lax.ppermute(array, axis, [(i, i ^ 1 << distance) for i in range(lax.axis...]
    ppermute x36 -> x0, starting transfers between devices: 71.4 us -> none  [swapped(): lax.ppermute(array, axis, [(i, i ^ 1 << distance) for i in range(lax.axis...]
    pallas_call x0 -> x1, Pallas kernels: none -> 50.1 us  [move(): pl.pallas_call(functools.partial(move_kernel, distance, bits), out_shape=...]
    concatenate x2, local copies, waits for them, and re-layouts: 0.17 us -> 35.8 us  [on_device(): jnp.concatenate([mixed, jnp.stack([top, total] * (mixed.shape[-1] // 2),...]
    all_gather x6 -> x0, blocking collectives: 31.6 us -> none  [joined(): lax.all_gather(part.astype(kind), axis)]
    gather x8 -> x4, local copies, waits for them, and re-layouts: 9.89 us -> 4.92 us  [partials(): stored = jax.vmap(lambda t, k: t[k], (0, 1), 1)(table, kept)]
    unnamed x24 -> x15, local copies, waits for them, and re-layouts: 5.53 us -> 1.26 us
    reduce_sum x5 -> x4, other arithmetic: 1.08 us -> 5 us  [the longest x1 3.83 us: finish(): jnp.sum(mixed * scale[..., None], axis=0)]
  transfers between devices with their start and end apart: 36 -> 1, of which waited for: 18 -> 1; matrix products, arithmetic and copies ran while one was open for 8% -> 1% of each run, Pallas kernels for 0% -> 0%
where the time goes in v1:
time: 128 us; the launch traced here: 127 us
  local copies, waits for them, and re-layouts  50.1 us (39%)
  Pallas kernels  50.1 us (39%)
  other arithmetic  10.9 us (9%)
  matrix products  6.96 us (5%)
  waiting for transfers between devices  3.68 us (3%)
  starting transfers between devices  3.41 us (3%)
  between operations  2.19 us (2%)
    pallas_call x1, Pallas kernels, move(): pl.pallas_call(functools.partial(move_kernel, distance, bits), out_shape=...  50.1 us
    concatenate x2, local copies, waits for them, and re-layouts, on_device(): jnp.concatenate([mixed, jnp.stack([top, total] * (mixed.shape[-1] // 2),...  35.8 us
    gather x4, local copies, waits for them, and re-layouts, partials(): stored = jax.vmap(lambda t, k: t[k], (0, 1), 1)(table, kept)  4.92 us
    dot_general x1, matrix products, partials(): jnp.einsum('srjgd,rptjd->srjgpt', q, view[:, :, :, 0], preferred_element_...  3.91 us
    reduce_sum x1, other arithmetic, finish(): jnp.sum(mixed * scale[..., None], axis=0)  3.83 us
    all_to_all x1, waiting for transfers between devices, on_device(): packed = lax.all_to_all(packed, 'blk', 2, 0, tiled=True)  3.68 us
    all_to_all x1, starting transfers between devices, on_device(): packed = lax.all_to_all(packed, 'blk', 2, 0, tiled=True)  3.41 us
    all_to_all x1, local copies, waits for them, and re-layouts, on_device(): packed = lax.all_to_all(packed, 'blk', 2, 0, tiled=True)  3.04 us
  transfers between devices with their start and end apart: 1, of which 1 were waited for; matrix products, arithmetic and copies ran while one was open for 1% of the time, Pallas kernels for 0%

profile of v1, /device:TPU:32, one launch (start us, length us, event | category | flops | bytes accessed | tf_op | source)
XLA Modules:
  0.0 127.4 jit_solution(10604715579987328530)
XLA Ops:
  0.6 0.0 copy-start
  0.7 0.7 fusion.22
  1.4 0.1 reshape.261
  1.5 0.0 copy-done
  1.5 0.0 copy-start.1
  1.5 4.8 %gather_fusion = s32[512]{0:T(512)S(1)} fusion(s32[2,64]{1,0:T(2,128)S(1)} %copy-done, s32[512]{0:T(512)S(1)} %reshape.261), kind=kCustom, calls=%fused_computation | custom fusion | bytes 8192 | tf_op jit(solution)/shard_map/vmap()/gather | solution.py:72
  6.2 0.1 reshape.264
  6.3 0.2 compare_reduce_fusion
  6.5 0.2 copy.1062
  6.7 0.0 copy-done.1
  6.7 0.6 copy.1297
  7.3 0.0 copy-start.2
  7.4 1.6 %fusion.34 = (bf16[2,16,16,1,8,128]{5,4,3,2,1,0:T(8,128)(2,1)}, bf16[2,16,16,1,8,128]{5,4,3,2,1,0:T(8,128)(2,1)S(1)}) fusion(bf16[2,16,16,2,8,128]{5,4,3,2,1,0:T(8,128)(2,1)S(1)} %bitcast.507), kind=kLoop, calls=%fused_computation.129 | loop fusion | bytes 4194304 | tf_op jit(solution)/shard_map/slice | solution.py:78
  8.9 0.0 copy-done.2
  8.9 0.1 reshape.257
  9.0 3.9 %fusion.1 = (f32[2,2,8,8]{3,0,2,1:T(2,128)S(1)}, f32[2,8,16,16,2,8]{3,5,4,2,1,0:T(8,128)S(1)}) fusion(pred[2,2,8,16]{0,3,2,1:T(8,128)(4,1)S(1)} %copy.1062, bf16[2,16,16,1,8,128]{5,4,3,2,1,0:T(8,128)(2,1)} %get-tuple-element.641, bf16[2,2,8,8,128]{4,3,2,1,0:T(8,128)(2,1)S(1)} %reshape.257), kind=kOutput, calls=%fused_computation.69 | convolution fusion | flops 16973568 | bytes 1377792 | tf_op jit(solution)/shard_map/srjgd,rptjd->srjgpt/dot_general | solution.py:77
  12.9 1.0 fusion.2
  14.0 2.6 %convolution_bitcast_fusion = f32[2,2,8,8,128]{4,3,0,2,1:T(8,128)S(1)} fusion(bf16[2,16,16,1,8,128]{5,4,3,2,1,0:T(8,128)(2,1)S(1)} %get-tuple-element.642, f32[2,8,16,16,2,8]{3,5,4,2,1,0:T(8,128)S(1)} %get-tuple-element.648, f32[2,2,8,8]{3,0,2,1:T(2,128)S(1)} %get-tuple-element.647, pred[2,2,8,16]{0,3,2,1:T(8,128)(4,1)S(1)} %copy.1062), kind=kOutput, calls=%fused_computation.72 | convolution fusion | flops 17104896 | bytes 1443328 | tf_op jit(solution)/shard_map/srjgpt,rptjd->srjgd/dot_general | solution.py:86
  16.5 0.3 copy.1070
  16.8 0.3 copy.1069
  17.1 35.1 %concatenate.3 = f32[2,2,8,8,256]{4,3,0,2,1:T(8,128)S(1)} concatenate(f32[2,2,8,8,128]{4,3,0,2,1:T(8,128)S(1)} %convolution_bitcast_fusion, f32[2,2,8,8,1]{4,3,0,2,1:T(8,128)S(1)} %copy.1069, f32[2,2,8,8,1]{4,3,0,2,1:T(8,128)S(1)} %copy.1070, f32[2,2,8,8,1]{4,3,0,2,1:T(8,128)S(1)} %copy.1069, f32[2,2,8,8,1]{4,3,0,2,1:T(8,128)S(1)} %copy.1070, f32[2,2,8,8,1]{4,3,0,2,1:T(8,128)S(1)} %copy.1069, ...), dimensions={4} | concatenate | bytes 524288 | tf_op jit(solution)/shard_map/concatenate | solution.py:133
  52.2 0.0 copy-start.3
  52.2 0.0 copy-start.4
  52.2 0.0 copy-start.5
  52.2 0.7 copy.1197
  52.9 3.4 %all-to-all-start = ((f32[2,2,8,8,256]{4,3,0,1,2:T(8,128)}), f32[2,2,8,8,256]{4,3,0,1,2:T(8,128)S(1)}, u32[]{:S(2)}, u32[]{:S(2)}) async-start(f32[2,2,8,8,256]{4,3,0,1,2:T(8,128)} %copy.1197), calls=%async_computation | async-start | bytes 524288 | tf_op jit(solution)/shard_map/all_to_all | solution.py:136
  56.4 0.1 slice.45
  56.5 0.0 copy-done.3
  56.5 0.0 copy-done.4
  56.5 0.0 copy-done.5
  56.5 0.6 fusion.35
  58.5 0.2 fusion.36
  58.7 3.7 %all-to-all-done = f32[2,2,8,8,256]{4,3,0,1,2:T(8,128)S(1)} async-done(((f32[2,2,8,8,256]{4,3,0,1,2:T(8,128)}), f32[2,2,8,8,256]{4,3,0,1,2:T(8,128)S(1)}, u32[]{:S(2)}, u32[]{:S(2)}) %all-to-all-start) | async-done | bytes 262176 | tf_op jit(solution)/shard_map/all_to_all | solution.py:136
  62.3 3.0 %copy.1199 = f32[2,2,4,2,8,256]{4,2,5,3,1,0:T(4,128)} copy(f32[2,2,4,2,8,256]{5,4,0,1,3,2:T(8,128)S(1)} %bitcast.508) | data formatting | bytes 524288 | tf_op jit(solution)/shard_map/all_to_all | solution.py:136
  65.4 0.7 slice_reduce_fusion.1
  66.1 0.8 fusion.33
  66.9 0.1 fusion.28
  67.1 3.8 %fusion = f32[2,2,2,8,128]{3,4,2,1,0:T(8,128)} fusion(f32[4,2,2,2,8,256]{4,0,5,3,2,1:T(4,128)} %bitcast.506, f32[4,2,2,2,8]{4,0,3,2,1:T(4,128)S(1)} %get-tuple-element.639), kind=kLoop, calls=%fused_computation.65 | loop fusion | flops 57344 | bytes 164864 | tf_op jit(solution)/shard_map/reduce_sum | solution.py:117
  70.9 1.2 copy.1209
  72.1 0.3 fusion.6
  72.4 50.8 %conditional.1 = (bf16[16,16,2048]{2,1,0:T(8,128)(2,1)}, bf16[1,2048]{1,0:T(2,128)(2,1)S(1)}) conditional(s32[]{:T(128)} %bitcast.28, (bf16[2,16,16,2048]{3,2,1,0:T(8,128)(2,1)S(1)}, bf16[16,128]{1,0:T(8,128)(2,1)S(1)}) %tuple.490, (bf16[2,16,16,2048]{3,2,1,0:T(8,128)(2,1)S(1)}, ...), branch_computations={%region_8.9_spmd, %region_9.10_spmd, %region_10.11_spmd, %region_1... | conditional | bytes 8208 | solution.py:141
  72.5 50.1 %branch_14_fun.1 = (bf16[16,16,2048]{2,1,0:T(8,128)(2,1)}, bf16[16,128]{1,0:T(8,128)(2,1)}) custom-call(bf16[2,16,16,2048]{3,2,1,0:T(8,128)(2,1)S(1)} %get-tuple-element.435.rows_ref, bf16[16,128]{1,0:T(8,128)(2,1)S(1)} %get-tuple-element.436.out_ref), custom_call_target="tpu_custom_call" | custom-call | tf_op jit(solution)/shard_map/cond/branch_14_fun/pallas_call | solution.py:55
  122.6 0.7 copy.1411
  123.3 1.4 %fusion.12 = bf16[1,16,16,2048]{3,2,1,0:T(8,128)(2,1)S(1)} fusion(bf16[16,16,2048]{2,1,0:T(8,128)(2,1)} %get-tuple-element.637, bf16[2,16,16,2048]{3,2,1,0:T(8,128)(2,1)S(1)} %copy-done.1, pred[]{:T(512)S(6)} %ne.3), kind=kLoop, calls=%fused_computation.85 | loop fusion | flops 524288 | bytes 3145729 | tf_op jit(solution)/shard_map/stack | solution.py:143
  124.6 0.6 copy.1462
  125.2 1.5 %pad_maximum_fusion = bf16[2,16,16,2048]{3,2,1,0:T(8,128)(2,1)} fusion(bf16[1,16,16,2048]{3,2,1,0:T(8,128)(2,1)S(1)} %slice.45, bf16[1,16,16,2048]{3,2,1,0:T(8,128)(2,1)S(1)} %fusion.12), kind=kLoop, calls=%fused_computation.66 | loop fusion | flops 1048576 | bytes 4194304 | tf_op jit(solution)/shard_map/stack | solution.py:143
  126.7 0.6 pad_maximum_fusion.1
  (18 shorter events, 0.2 us)
Async XLA Ops:
  0.6 0.8 copy-start
  1.5 5.2 %copy-start.1 = (bf16[2,16,16,2048]{3,2,1,0:T(8,128)(2,1)S(1)}, bf16[2,16,16,2048]{3,2,1,0:T(8,128)(2,1)}, u32[]{:S(2)}) copy-start(bf16[2,16,16,2048]{3,2,1,0:T(8,128)(2,1)} %param.73) | copy-start | bytes 6291460
  7.3 1.6 %copy-start.2 = (bf16[2,2,8192]{2,1,0:T(2,128)(2,1)S(1)}, bf16[2,2,8192]{2,1,0:T(2,128)(2,1)}, u32[]{:S(2)}) copy-start(bf16[2,2,8192]{2,1,0:T(2,128)(2,1)} %param.70) | copy-start | bytes 196612
  52.2 4.3 %copy-start.3 = (bf16[2,2,1024]{2,1,0:T(2,128)(2,1)S(1)}, bf16[2,2,1024]{2,1,0:T(2,128)(2,1)}, u32[]{:S(2)}) copy-start(bf16[2,2,1024]{2,1,0:T(2,128)(2,1)} %param.71) | copy-start | bytes 24580
  52.2 4.3 %copy-start.4 = (bf16[2,2,1024]{2,1,0:T(2,128)(2,1)S(1)}, bf16[2,2,1024]{2,1,0:T(2,128)(2,1)}, u32[]{:S(2)}) copy-start(bf16[2,2,1024]{2,1,0:T(2,128)(2,1)} %param.72) | copy-start | bytes 24580
  52.2 4.3 %copy-start.5 = (s32[64]{0:T(128)S(1)}, s32[64]{0:T(128)}, u32[]{:S(2)}) copy-start(s32[64]{0:T(128)} %param.76) | copy-start | bytes 772
  52.9 9.4 %all-to-all-start = ((f32[2,2,8,8,256]{4,3,0,1,2:T(8,128)}), f32[2,2,8,8,256]{4,3,0,1,2:T(8,128)S(1)}, u32[]{:S(2)}, u32[]{:S(2)}) async-start(f32[2,2,8,8,256]{4,3,0,1,2:T(8,128)} %copy.1197), calls=%async_computation | async-start | bytes 524288 | tf_op jit(solution)/shard_map/all_to_all | solution.py:136

commit v2 on v1

v2 whole, which is shorter than its diff:
```python
import functools

import jax
import jax.numpy as jnp
from jax import lax
from jax.experimental import pallas as pl
from jax.experimental.pallas import tpu as pltpu
from jax.sharding import PartitionSpec as P

NEG = -1e30
MESH = pl.DeviceIdType.MESH
F32, BF16 = jnp.float32, jnp.bfloat16
LANES = 128


def partner_of(index, distance, bits):
    other = 0
    for bit in range(bits):
        value = (index // (1 << bit)) % 2
        if (distance >> bit) & 1:
            value = 1 - value
        other = other + value * (1 << bit)
    return other


def lanes_at(start):
    return pl.ds(pl.multiple_of(start * LANES, LANES), LANES)


def fused_kernel(
    distance, bits,
    moves, cache, queries, keys, values, table, kept,
    got_rows, first_out, second_out,
    cache_v, q_raw, k_raw, v_raw, table_s, kept_s, first_v, second_v,
    q_all, sent, came, o_all, row_send, row_got,
    load_sem, store_sem, big_sem, part_ss, part_rs, row_sem,
):
    g = lax.axis_index("req")
    blk = lax.axis_index("blk")
    blks = sent.shape[0]
    rows, pages, size, _ = cache_v.shape
    heads = q_all.shape[0]
    steps, keep = kept_s.shape[0], kept_s.shape[3]
    own = heads // blks
    both = q_all.shape[2]
    group = both // steps
    tokens = pages * size
    scale = LANES**-0.5
    there = {"req": partner_of(g, distance, bits)}

    barrier = pltpu.get_barrier_semaphore()
    pl.semaphore_signal(barrier, inc=1, device_id=there, device_id_type=MESH)

    def greet(rel, carry):
        peer = {"blk": lax.rem(blk + rel, blks)}
        pl.semaphore_signal(barrier, inc=1, device_id=peer, device_id_type=MESH)
        return carry

    lax.fori_loop(1, blks, greet, 0)
    loads = [
        pltpu.make_async_copy(src, dst, load_sem.at[i])
        for i, (src, dst) in enumerate(
            [
                (table, table_s),
                (kept, kept_s),
                (queries, q_raw),
                (keys, k_raw),
                (values, v_raw),
                (cache, cache_v),
            ]
        )
    ]
    for load in loads:
        load.start()
    pl.semaphore_wait(barrier, blks)

    big = pltpu.make_async_remote_copy(
        src_ref=cache.at[0],
        dst_ref=got_rows,
        send_sem=big_sem.at[0],
        recv_sem=big_sem.at[1],
        device_id=there,
        device_id_type=MESH,
    )
    big.start()
    for load in loads:
        load.wait()

    sent[...] = jnp.zeros_like(sent)
    lane = lax.broadcasted_iota(jnp.int32, (both, LANES), 1)
    place = lax.broadcasted_iota(jnp.int32, (both, tokens), 1) // size + blk * pages
    early = lax.broadcasted_iota(jnp.int32, (both, tokens), 0) < group

    def head(j, carry):
        def spread(i, inner):
            pair = q_raw[i // group, :, lanes_at(j * group + i % group)].astype(F32)
            for r in range(rows):
                q_all[j, r, pl.ds(i, 1), :] = pair[r : r + 1]
            return inner

        lax.fori_loop(0, both, spread, 0)

        def request(r, inner):
            def mark(k, found):
                first, second = (table_s[r, kept_s[s, r, j, k]] for s in range(steps))
                return jnp.where(place == jnp.where(early, first, second), 1.0, found)

            live = lax.fori_loop(0, keep, mark, jnp.zeros((both, tokens), F32)) > 0.0
            k = cache_v[r, :, :, lanes_at(j)].reshape(tokens, LANES)
            v = cache_v[r, :, :, lanes_at(j + heads)].reshape(tokens, LANES)
            scores = lax.dot_general(
                q_all[j, r].astype(BF16), k, (((1,), (1,)), ((), ())), preferred_element_type=F32
            )
            scores = jnp.where(live, scores * scale, NEG)
            top = jnp.max(scores, axis=1, keepdims=True)
            weights = jnp.where(live, jnp.exp(scores - top), 0.0)
            total = jnp.sum(weights, axis=1, keepdims=True)
            to, at = j // own, (j % own) * rows + r
            sent[to, at] = jnp.dot(weights.astype(BF16), v, preferred_element_type=F32)
            old = sent[to, own * rows]
            sent[to, own * rows] = jnp.where(
                lane == at, top, jnp.where(lane == at + LANES // 2, total, old)
            )
            return inner

        lax.fori_loop(0, rows, request, 0)
        return carry

    lax.fori_loop(0, heads, head, 0)

    def part(rel):
        to = lax.rem(blk + rel, blks)
        return pltpu.make_async_remote_copy(
            src_ref=sent.at[to],
            dst_ref=came.at[rel],
            send_sem=part_ss.at[rel],
            recv_sem=part_rs.at[rel],
            device_id={"blk": to},
            device_id_type=MESH,
        )

    def each_part(act):
        def one(rel, carry):
            act(part(rel))
            return carry

        lax.fori_loop(1, blks, one, 0)

    each_part(lambda copy: copy.start())
    came[0] = sent[blk]
    each_part(lambda copy: copy.wait_recv())

    late = lax.broadcasted_iota(jnp.int32, (both, 1), 0) >= group

    def merge(at, carry):
        r = at % rows
        j = blk * own + at // rows

        def pick(raw, n):
            pair = raw[n, :, lanes_at(j)].astype(F32)
            return jnp.where(r == 0, pair[0:1], pair[1:2])

        def column(i, place):
            kept_lane = jnp.where(lane == place, came[i, own * rows], 0.0)
            return jnp.sum(kept_lane, axis=1, keepdims=True)

        query = q_all[j, r]
        fresh = [
            jnp.sum(query * pick(k_raw, n), axis=1, keepdims=True) * scale for n in range(steps)
        ]
        fresh[1] = jnp.where(late, fresh[1], NEG)
        tops = [column(i, at) for i in range(blks)]
        best = functools.reduce(jnp.maximum, tops + fresh)
        total = jnp.zeros_like(best)
        mixed = jnp.zeros((both, LANES), F32)
        for i, top in enumerate(tops):
            factor = jnp.exp(top - best)
            total = total + factor * column(i, at + LANES // 2)
            mixed = mixed + factor * came[i, at]
        for n, score in enumerate(fresh):
            weight = jnp.exp(score - best)
            if n:
                weight = jnp.where(late, weight, 0.0)
            total = total + weight
            mixed = mixed + weight.astype(BF16).astype(F32) * pick(v_raw, n)
        o_all[at] = mixed / total
        return carry

    lax.fori_loop(0, own * rows, merge, 0)

    for jj in range(own):
        row_send[jj * group : (jj + 1) * group] = o_all[jj * rows, group:both]
    row_copy = pltpu.make_async_remote_copy(
        src_ref=row_send,
        dst_ref=row_got,
        send_sem=row_sem.at[0],
        recv_sem=row_sem.at[1],
        device_id=there,
        device_id_type=MESH,
    )
    row_copy.start()

    def lay_first(i, carry):
        at = (i // group) * rows
        first_v[:, lanes_at(i)] = jnp.concatenate(
            [o_all[at + r, pl.ds(i % group, 1), :] for r in range(rows)], axis=0
        ).astype(BF16)
        return carry

    lax.fori_loop(0, own * group, lay_first, 0)
    first_copy = pltpu.make_async_copy(first_v, first_out, store_sem.at[0])
    first_copy.start()
    each_part(lambda copy: copy.wait_send())
    row_copy.wait()
    moving = moves[g] != g

    def lay_second(i, carry):
        at = (i // group) * rows
        moved = jnp.where(moving, row_got[pl.ds(i, 1), :], row_send[pl.ds(i, 1), :])
        stays = o_all[at + 1, pl.ds(i % group + group, 1), :]
        second_v[:, lanes_at(i)] = jnp.concatenate([moved, stays], axis=0).astype(BF16)
        return carry

    lax.fori_loop(0, own * group, lay_second, 0)
    second_copy = pltpu.make_async_copy(second_v, second_out, store_sem.at[1])
    second_copy.start()
    first_copy.wait()
    second_copy.wait()
    big.wait()


def fused(distance, bits, moves, cache, queries, keys, values, table, kept):
    steps, rows, heads, keep = kept.shape
    pages, size, width = cache.shape[1:]
    blks = lax.axis_size("blk")
    own = heads // blks
    group = queries.shape[2] // (heads * LANES)
    both = steps * group
    anywhere = pl.BlockSpec(memory_space=pl.ANY)
    out = jax.ShapeDtypeStruct((rows, own * group * LANES), BF16)
    dma = pltpu.SemaphoreType.DMA
    return pl.pallas_call(
        functools.partial(fused_kernel, distance, bits),
        out_shape=(jax.ShapeDtypeStruct(cache.shape[1:], cache.dtype), out, out),
        in_specs=[pl.BlockSpec(memory_space=pltpu.SMEM)] + [anywhere] * 6,
        out_specs=(anywhere,) * 3,
        scratch_shapes=[
            pltpu.VMEM(cache.shape, BF16),
            pltpu.VMEM(queries.shape, BF16),
            pltpu.VMEM(keys.shape, BF16),
            pltpu.VMEM(values.shape, BF16),
            pltpu.SMEM(table.shape, jnp.int32),
            pltpu.SMEM(kept.shape, jnp.int32),
            pltpu.VMEM(out.shape, BF16),
            pltpu.VMEM(out.shape, BF16),
            pltpu.VMEM((heads, rows, both, LANES), F32),
            pltpu.VMEM((blks, own * rows + 1, both, LANES), F32),
            pltpu.VMEM((blks, own * rows + 1, both, LANES), F32),
            pltpu.VMEM((own * rows, both, LANES), F32),
            pltpu.VMEM((own * group, LANES), F32),
            pltpu.VMEM((own * group, LANES), F32),
            dma((6,)),
            dma((2,)),
            dma((2,)),
            dma((blks,)),
            dma((blks,)),
            dma((2,)),
        ],
        compiler_params=pltpu.CompilerParams(
            collective_id=distance, has_side_effects=True, vmem_limit_bytes=48 << 20
        ),
        name="attend_and_move",
    )(moves, cache, queries, keys, values, table, kept)


def on_device(queries, new_keys, new_values, cache, page_table, kept, moves):
    count = lax.axis_size("req")
    bits = count.bit_length() - 1
    branches = [functools.partial(fused, d, bits) for d in range(1, count)]
    got, first, second = lax.switch(
        moves[0] - 1, branches, moves, cache, queries, new_keys, new_values, page_table, kept
    )
    g = lax.axis_index("req")
    first_row = lax.broadcasted_iota(jnp.int32, (cache.shape[0], 1, 1, 1), 0) == 0
    arrives = jnp.logical_and(moves[g] != g, first_row)
    return first, second, jnp.where(arrives, got[None], cache)


def solution(mesh):
    in_specs = (
        P(None, "req", None),
        P(None, "req", None),
        P(None, "req", None),
        P("req", "blk", None, None),
        P("req", None),
        P(None, "req", None, None),
        P(),
    )
    out_specs = (P("req", "blk"), P("req", "blk"), P("req", "blk", None, None))
    return jax.shard_map(
        on_device, mesh=mesh, in_specs=in_specs, out_specs=out_specs, check_vma=False
    )
```

time: 128 us -> 64.1 us (0.50)
  the two profiles are of different devices: /device:TPU:32 before, /device:TPU:1 now
where the time goes in v2:
time: 64.1 us; the launch traced here: 63.9 us
  Pallas kernels  55.7 us (87%)
  other arithmetic  3.2 us (5%)
  local copies, waits for them, and re-layouts  2.52 us (4%)
  between operations  1.95 us (3%)
    pallas_call x1, Pallas kernels, fused(): pl.pallas_call(functools.partial(fused_kernel, distance, bits), out_shape...  55.7 us
    select_n x1, other arithmetic, on_device(): return (first, second, jnp.where(arrives, got[None], cache))  3.19 us
    dynamic_slice x1, local copies, waits for them, and re-layouts, on_device(): arrives = jnp.logical_and(moves[g] != g, first_row)  1.32 us

profile of v2, /device:TPU:1, one launch (start us, length us, event | category | flops | bytes accessed | tf_op | source)
XLA Modules:
  0.0 63.9 jit_solution(14334948640212704827)
XLA Ops:
  0.6 1.3 %fusion = (s32[1]{0:T(128)}, s32[1]{0:T(128)}) fusion(s32[64]{0:T(128)} %param.76, s32[]{:T(128)S(6)} %select_n.7), kind=kLoop, calls=%fused_computation.2 | loop fusion | bytes 20 | tf_op jit(solution)/shard_map/dynamic_slice | solution.py:285
  3.3 56.2 %conditional.1 = ((bf16[16,16,2048]{2,1,0:T(8,128)(2,1)S(1)}, bf16[2,2048]{1,0:T(2,128)(2,1)S(1)}, bf16[2,2048]{1,0:T(2,128)(2,1)S(1)})) conditional(s32[]{:T(128)} %bitcast, (s32[64]{0:T(128)}, bf16[2,16,16,2048]{3,2,1,0:T(8,128)(2,1)}, bf16[2,2,8192]{2,1,0:T(2,128)(2,1)}, bf16[2,2,1024]{2,1,0:T(2,128)(2,1)}, ...), branch_computations={%region_0.0_spmd, %region_1.0_spmd, %region_2.0_spmd, %region_3.0_... | conditional | bytes 8 | solution.py:280
  3.3 55.7 %attend_and_move.72 = (bf16[16,16,2048]{2,1,0:T(8,128)(2,1)S(1)}, bf16[2,2048]{1,0:T(2,128)(2,1)S(1)}, bf16[2,2048]{1,0:T(2,128)(2,1)S(1)}) custom-call(s32[64]{0:T(128)} %get-tuple-element.945.moves, bf16[2,16,16,2048]{3,2,1,0:T(8,128)(2,1)} %get-tuple-element.946.cache, bf16[2,2,8192]{2,1,0:T(2,128)(2,1)} %get-tuple-element.947.queries, ...), custom_call_target="tpu_custom_call" | custom-call | tf_op jit(solution)/shard_map/cond/branch_9_fun/attend_and_move/pallas_call | solution.py:242
  59.5 3.2 %broadcast_select_fusion = bf16[2,16,16,2048]{3,2,1,0:T(8,128)(2,1)} fusion(bf16[2,16,16,2048]{3,2,1,0:T(8,128)(2,1)} %param.73, pred[2]{0:T(512)(128)(4,1)S(1)} %compare_and_fusion, bf16[16,16,2048]{2,1,0:T(8,128)(2,1)S(1)} %get-tuple-element.1331), kind=kLoop, calls=%fused_computation | loop fusion | flops 1048576 | bytes 5242882 | tf_op jit(solution)/shard_map/jit(_where)/select_n | solution.py:286
  62.7 0.6 copy.201
  63.3 0.6 copy.202
  (1 shorter events, 0.0 us)

commit v3 on v2

v3 whole, which is shorter than its diff:
```python
import functools

import jax
import jax.numpy as jnp
from jax import lax
from jax.experimental import pallas as pl
from jax.experimental.pallas import tpu as pltpu
from jax.sharding import PartitionSpec as P

NEG = -1e30
MESH = pl.DeviceIdType.MESH
F32, BF16 = jnp.float32, jnp.bfloat16
LANES = 128
PHASES = (6, 7, 3)


def partner_of(index, distance, bits):
    other = index
    for bit in range(bits):
        if (distance >> bit) & 1:
            value = lax.rem(lax.div(index, 1 << bit), 2)
            other = other + (1 << bit) - value * (2 << bit)
    return other


def in_parts(distance):
    return distance // 32 == 1 and distance // 4 % 8 < 2


def lanes_at(start):
    return pl.ds(pl.multiple_of(start * LANES, LANES), LANES)


def fused_kernel(
    distance, bits,
    cache, queries, keys, values, table, kept,
    got_rows, stage, heads_out, moved_out,
    cache_v, q_raw, k_raw, v_raw, table_s, kept_s,
    q_all, sent, came, o_all,
    load_sem, store_sem, big_sem, part_ss, part_rs, row_sem,
):
    g = lax.axis_index("req")
    blk = lax.axis_index("blk")
    blks = sent.shape[0]
    rows, pages, size, _ = cache_v.shape
    heads = q_all.shape[0]
    steps, keep = kept_s.shape[0], kept_s.shape[3]
    own = heads // blks
    both = q_all.shape[2]
    group = both // steps
    tokens = pages * size
    scale = LANES**-0.5
    there = {"req": partner_of(g, distance, bits)}

    barrier = pltpu.get_barrier_semaphore()
    pl.semaphore_signal(barrier, inc=1, device_id=there, device_id_type=MESH)

    def greet(rel, carry):
        peer = {"blk": lax.rem(blk + rel, blks)}
        pl.semaphore_signal(barrier, inc=1, device_id=peer, device_id_type=MESH)
        return carry

    lax.fori_loop(1, blks, greet, 0)
    loads = [
        pltpu.make_async_copy(src, dst, load_sem.at[i])
        for i, (src, dst) in enumerate(
            [
                (table, table_s),
                (kept, kept_s),
                (queries, q_raw),
                (keys, k_raw),
                (values, v_raw),
                (cache, cache_v),
            ]
        )
    ]
    for load in loads:
        load.start()
    pl.semaphore_wait(barrier, blks)

    sizes = PHASES if in_parts(distance) else (pages,)
    edges = [sum(sizes[:i]) for i in range(len(sizes))]
    big = [
        pltpu.make_async_remote_copy(
            src_ref=cache.at[0, pl.ds(edge, length)],
            dst_ref=got_rows.at[pl.ds(edge, length)],
            send_sem=big_sem.at[0, i],
            recv_sem=big_sem.at[1, i],
            device_id=there,
            device_id_type=MESH,
        )
        for i, (edge, length) in enumerate(zip(edges, sizes))
    ]
    big[0].start()
    for load in loads:
        load.wait()
    stage_copy = pltpu.make_async_copy(cache, stage, store_sem.at[0])
    stage_copy.start()

    for i in range(blks):
        sent[i, own * rows] = jnp.zeros((both, LANES), F32)
    def part(rel):
        to = lax.rem(blk + rel, blks)
        return pltpu.make_async_remote_copy(
            src_ref=sent.at[to],
            dst_ref=came.at[rel],
            send_sem=part_ss.at[rel],
            recv_sem=part_rs.at[rel],
            device_id={"blk": to},
            device_id_type=MESH,
        )

    lane = lax.broadcasted_iota(jnp.int32, (both, LANES), 1)
    place = lax.broadcasted_iota(jnp.int32, (both, tokens), 1) // size + blk * pages
    early = lax.broadcasted_iota(jnp.int32, (both, tokens), 0) < group

    def head(j, carry):
        def spread(i, inner):
            pair = q_raw[i // group, :, lanes_at(j * group + i % group)].astype(F32)
            for r in range(rows):
                q_all[j, r, pl.ds(i, 1), :] = pair[r : r + 1]
            return inner

        lax.fori_loop(0, both, spread, 0)

        def request(r, inner):
            def mark(k, found):
                first, second = (table_s[r, kept_s[s, r, j, k]] for s in range(steps))
                return jnp.where(place == jnp.where(early, first, second), 1.0, found)

            live = lax.fori_loop(0, keep, mark, jnp.zeros((both, tokens), F32)) > 0.0
            k = cache_v[r, :, :, lanes_at(j)].reshape(tokens, LANES)
            v = cache_v[r, :, :, lanes_at(j + heads)].reshape(tokens, LANES)
            scores = lax.dot_general(
                q_all[j, r].astype(BF16), k, (((1,), (1,)), ((), ())), preferred_element_type=F32
            )
            scores = jnp.where(live, scores * scale, NEG)
            top = jnp.max(scores, axis=1, keepdims=True)
            weights = jnp.where(live, jnp.exp(scores - top), 0.0)
            total = jnp.sum(weights, axis=1, keepdims=True)
            to, at = j // own, (j % own) * rows + r
            sent[to, at] = jnp.dot(weights.astype(BF16), v, preferred_element_type=F32)
            old = sent[to, own * rows]
            sent[to, own * rows] = jnp.where(
                lane == at, top, jnp.where(lane == at + LANES // 2, total, old)
            )
            return inner

        lax.fori_loop(0, rows, request, 0)
        return carry

    def block(rel, carry):
        to = lax.rem(blk + rel, blks)
        lax.fori_loop(to * own, to * own + own, head, 0)

        @pl.when(rel < blks)
        def _():
            part(rel).start()

        return carry

    lax.fori_loop(1, blks + 1, block, 0)
    for copy in big[1:2]:
        copy.start()
    came[0] = sent[blk]

    def arrive(rel, carry):
        part(rel).wait()
        return carry

    lax.fori_loop(1, blks, arrive, 0)

    late = lax.broadcasted_iota(jnp.int32, (both, 1), 0) >= group

    def merge(at, carry):
        r = at % rows
        j = blk * own + at // rows

        def pick(raw, n):
            pair = raw[n, :, lanes_at(j)].astype(F32)
            return jnp.where(r == 0, pair[0:1], pair[1:2])

        def column(i, place):
            kept_lane = jnp.where(lane == place, came[i, own * rows], 0.0)
            return jnp.sum(kept_lane, axis=1, keepdims=True)

        query = q_all[j, r]
        fresh = [
            jnp.sum(query * pick(k_raw, n), axis=1, keepdims=True) * scale for n in range(steps)
        ]
        fresh[1] = jnp.where(late, fresh[1], NEG)
        best = jnp.maximum(*fresh)
        weights = [jnp.exp(score - best) for score in fresh]
        weights[1] = jnp.where(late, weights[1], 0.0)
        mixed = sum(
            weight.astype(BF16).astype(F32) * pick(v_raw, n) for n, weight in enumerate(weights)
        )

        def fold(i, state):
            best, total, mixed = state
            top = column(i, at)
            new = jnp.maximum(best, top)
            past, factor = jnp.exp(best - new), jnp.exp(top - new)
            total = total * past + column(i, at + LANES // 2) * factor
            return new, total, mixed * past + came[i, at] * factor

        _, total, mixed = lax.fori_loop(0, blks, fold, (best, weights[0] + weights[1], mixed))
        o_all[at // rows, r] = mixed / total
        return carry

    lax.fori_loop(0, own * rows, merge, 0)

    row_copy = pltpu.make_async_remote_copy(
        src_ref=o_all.at[:, 0, pl.ds(group, group)],
        dst_ref=moved_out,
        send_sem=row_sem.at[0],
        recv_sem=row_sem.at[1],
        device_id=there,
        device_id_type=MESH,
    )
    row_copy.start()
    for copy in big[2:]:
        copy.start()
    heads_copy = pltpu.make_async_copy(o_all, heads_out, store_sem.at[1])
    heads_copy.start()
    stage_copy.wait()
    heads_copy.wait()
    row_copy.wait()
    for copy in big:
        copy.wait()


def fused(distance, bits, cache, queries, keys, values, table, kept):
    steps, rows, heads, keep = kept.shape
    pages, size, width = cache.shape[1:]
    blks = lax.axis_size("blk")
    own = heads // blks
    group = queries.shape[2] // (heads * LANES)
    both = steps * group
    anywhere = pl.BlockSpec(memory_space=pl.ANY)
    dma = pltpu.SemaphoreType.DMA
    return pl.pallas_call(
        functools.partial(fused_kernel, distance, bits),
        out_shape=(
            jax.ShapeDtypeStruct(cache.shape[1:], cache.dtype),
            jax.ShapeDtypeStruct(cache.shape, cache.dtype),
            jax.ShapeDtypeStruct((own, rows, both, LANES), F32),
            jax.ShapeDtypeStruct((own, group, LANES), F32),
        ),
        in_specs=[anywhere] * 6,
        out_specs=(anywhere,) * 4,
        scratch_shapes=[
            pltpu.VMEM(cache.shape, BF16),
            pltpu.VMEM(queries.shape, BF16),
            pltpu.VMEM(keys.shape, BF16),
            pltpu.VMEM(values.shape, BF16),
            pltpu.SMEM(table.shape, jnp.int32),
            pltpu.SMEM(kept.shape, jnp.int32),
            pltpu.VMEM((heads, rows, both, LANES), F32),
            pltpu.VMEM((blks, own * rows + 1, both, LANES), F32),
            pltpu.VMEM((blks, own * rows + 1, both, LANES), F32),
            pltpu.VMEM((own, rows, both, LANES), F32),
            dma((6,)),
            dma((2,)),
            dma((2, len(PHASES) if in_parts(distance) else 1)),
            dma((blks,)),
            dma((blks,)),
            dma((2,)),
        ],
        compiler_params=pltpu.CompilerParams(
            collective_id=distance, has_side_effects=True, vmem_limit_bytes=48 << 20
        ),
        name="attend_and_move",
    )(cache, queries, keys, values, table, kept)


def settle_kernel(
    moves, got, stage, heads_out, moved_out,
    after, first_out, second_out,
    moves_s, heads_v, moved_v, first_v, second_v, load_sem, store_sem,
):
    g = lax.axis_index("req")
    own, rows, both, _ = heads_v.shape
    group = moved_v.shape[1]
    loads = [
        pltpu.make_async_copy(src, dst, load_sem.at[i])
        for i, (src, dst) in enumerate(
            [(moves, moves_s), (heads_out, heads_v), (moved_out, moved_v)]
        )
    ]
    stays = pltpu.make_async_copy(stage.at[1], after.at[1], store_sem.at[0])
    keeps = pltpu.make_async_copy(stage.at[0], after.at[0], store_sem.at[1])
    renews = pltpu.make_async_copy(got, after.at[0], store_sem.at[1])
    for load in loads:
        load.start()
    stays.start()
    loads[0].wait()
    moving = moves_s[g] != g

    @pl.when(moving)
    def _():
        renews.start()

    @pl.when(jnp.logical_not(moving))
    def _():
        keeps.start()

    loads[1].wait()
    loads[2].wait()
    for jj in range(own):
        for q in range(group):
            lanes = pl.ds((jj * group + q) * LANES, LANES)
            late = group + q
            moved = jnp.where(moving, moved_v[jj, q : q + 1], heads_v[jj, 0, late : late + 1])
            first_v[:, lanes] = jnp.concatenate(
                [heads_v[jj, r, q : q + 1] for r in range(rows)], axis=0
            ).astype(BF16)
            second_v[:, lanes] = jnp.concatenate(
                [moved, heads_v[jj, 1, late : late + 1]], axis=0
            ).astype(BF16)
    out = [
        pltpu.make_async_copy(first_v, first_out, store_sem.at[2]),
        pltpu.make_async_copy(second_v, second_out, store_sem.at[3]),
    ]
    for copy in out:
        copy.start()
    stays.wait()
    keeps.wait()
    for copy in out:
        copy.wait()


def settle(moves, got, stage, heads_out, moved_out):
    own, rows, both, _ = heads_out.shape
    out = jax.ShapeDtypeStruct((rows, own * moved_out.shape[1] * LANES), BF16)
    anywhere = pl.BlockSpec(memory_space=pl.ANY)
    return pl.pallas_call(
        settle_kernel,
        out_shape=(jax.ShapeDtypeStruct(stage.shape, stage.dtype), out, out),
        in_specs=[anywhere] * 5,
        out_specs=(anywhere,) * 3,
        scratch_shapes=[
            pltpu.SMEM(moves.shape, jnp.int32),
            pltpu.VMEM(heads_out.shape, F32),
            pltpu.VMEM(moved_out.shape, F32),
            pltpu.VMEM(out.shape, BF16),
            pltpu.VMEM(out.shape, BF16),
            pltpu.SemaphoreType.DMA((3,)),
            pltpu.SemaphoreType.DMA((4,)),
        ],
        compiler_params=pltpu.CompilerParams(vmem_limit_bytes=32 << 20),
        name="settle",
    )(moves, got, stage, heads_out, moved_out)


def on_device(queries, new_keys, new_values, cache, page_table, kept, moves):
    count = lax.axis_size("req")
    bits = count.bit_length() - 1
    branches = [functools.partial(fused, d, bits) for d in range(1, count)]
    pieces = lax.switch(
        moves[0] - 1, branches, cache, queries, new_keys, new_values, page_table, kept
    )
    after, first, second = settle(moves, *pieces)
    return first, second, after


def solution(mesh):
    in_specs = (
        P(None, "req", None),
        P(None, "req", None),
        P(None, "req", None),
        P("req", "blk", None, None),
        P("req", None),
        P(None, "req", None, None),
        P(),
    )
    out_specs = (P("req", "blk"), P("req", "blk"), P("req", "blk", None, None))
    return jax.shard_map(
        on_device, mesh=mesh, in_specs=in_specs, out_specs=out_specs, check_vma=False
    )
```

time: 64.1 us -> 58.2 us (0.908)
  the two profiles are of different devices: /device:TPU:1 before, /device:TPU:32 now
where the time goes in v3:
time: 58.2 us; the launch traced here: 58 us
  Pallas kernels  56.3 us (97%)
  between operations  1.46 us (3%)
    pallas_call x1, Pallas kernels, fused(): pl.pallas_call(functools.partial(fused_kernel, distance, bits), out_shape...  54.7 us
    pallas_call x1, Pallas kernels, settle(): pl.pallas_call(settle_kernel, out_shape=(jax.ShapeDtypeStruct(stage.shape...  1.58 us

profile of v3, /device:TPU:32, one launch (start us, length us, event | category | flops | bytes accessed | tf_op | source)
XLA Modules:
  0.0 58.0 jit_solution(15390282319739910610)
XLA Ops:
  1.3 0.0 copy-start
  1.3 55.0 %conditional.1 = ((bf16[16,16,2048]{2,1,0:T(8,128)(2,1)S(1)}, bf16[2,16,16,2048]{3,2,1,0:T(8,128)(2,1)S(1)}, f32[2,2,16,128]{3,2,1,0:T(8,128)S(1)}, f32[2,8,128]{2,1,0:T(8,128)S(1)})) conditional(s32[]{:T(128)} %bitcast, (bf16[2,16,16,2048]{3,2,1,0:T(8,128)(2,1)}, bf16[2,2,8192]{2,1,0:T(2,128)(2,1)}, ...), branch_computations={%region_0.0_spmd, %region_1.0_spmd, %region_2.0_spmd, %region_3.0_... | conditional | bytes 8 | solution.py:360
  1.3 54.7 %attend_and_move.78 = (bf16[16,16,2048]{2,1,0:T(8,128)(2,1)S(1)}, bf16[2,16,16,2048]{3,2,1,0:T(8,128)(2,1)S(1)}, f32[2,2,16,128]{3,2,1,0:T(8,128)S(1)}, f32[2,8,128]{2,1,0:T(8,128)S(1)}) custom-call(bf16[2,16,16,2048]{3,2,1,0:T(8,128)(2,1)} %get-tuple-element.846.cache, bf16[2,2,8192]{2,1,0:T(2,128)(2,1)} %get-tuple-element.847.queries, ...), custom_call_target="tpu_custom_call" | custom-call | tf_op jit(solution)/shard_map/cond/branch_15_fun/attend_and_move/pallas_call | solution.py:242
  56.3 0.0 copy-done
  56.3 1.6 %settle.1 = (bf16[2,16,16,2048]{3,2,1,0:T(8,128)(2,1)}, bf16[2,2048]{1,0:T(2,128)(2,1)}, bf16[2,2048]{1,0:T(2,128)(2,1)}) custom-call(s32[64]{0:T(128)S(1)} %copy-done, bf16[16,16,2048]{2,1,0:T(8,128)(2,1)S(1)} %get-tuple-element.1144.got, bf16[2,16,16,2048]{3,2,1,0:T(8,128)(2,1)S(1)} %get-tuple-element.1145.stage, ...), custom_call_target="tpu_custom_call" | custom-call | tf_op jit(solution)/shard_map/settle/pallas_call | solution.py:337
Async XLA Ops:
  1.3 55.0 %copy-start = (s32[64]{0:T(128)S(1)}, s32[64]{0:T(128)}, u32[]{:S(2)}) copy-start(s32[64]{0:T(128)} %moves.1) | copy-start | bytes 772
